TPU v7x, 32 devices: a whole 2x2x4 slice. The times are simulated.
32 devices in a mesh: scen: 4 (over z), net: 8 (over y, x, core).
Axes of the slice: x: 2, y: 2, z: 4, core: 2. Of those that a mesh axis runs over, the one named last changes fastest.
Arguments:
- coupling: bfloat16 [768, 64, 320], P('net'), may hold values from -0.3125 to 0.3125
- tie_blocks: bfloat16 [1024, 64, 128], P('net'), may hold values from -0.5 to 0.5
- w_pattern: int32 [768, 4], P('net'), may hold values from 0 to 127
- link_pattern: int32 [768], P('net'), may hold values from 0 to 127
- left_bounds: int32 [1024], P('net'), may hold values from 0 to 127
- right_bounds: int32 [1024], P('net'), may hold values from 0 to 127
- block_counts: int32 [8], P('net'), may hold values from 48 to 96, as said below
- commit_cost: float32 [1024, 64], P('net'), may hold values from -3 to 3
- dispatch_cost: float32 [1024, 64], P('net'), may hold values from -6 to 6
- demand: float32 [768, 64], P('net'), may hold values from -6 to 6
- wind_error: bfloat16 [768, 64, 512], P('net', None, 'scen'), may hold values from -3 to 3
- commit_start: float32 [1024, 64], P('net'), may hold values from 0 to 1
- dispatch_start: float32 [1024, 64, 512], P('net', None, 'scen'), may hold values from 0 to 2
- dual_start: float32 [768, 64, 512], P('net', None, 'scen'), may hold values from -8 to 8
- tie_start: float32 [1024, 64, 512], P('net', None, 'scen'), may hold values from -6 to 6
Outputs:
- commit_out: float32 [1024, 64], P('net')
- dispatch_out: float32 [1024, 64, 512], P('net', None, 'scen')
- dual_out: float32 [768, 64, 512], P('net', None, 'scen')
- tie_out: float32 [1024, 64, 512], P('net', None, 'scen')
Inputs may be any that keep to these rules, and one draw needn't show every extreme that they name: `block_counts`: some partition has all 96 row blocks active.
All inputs are finite; a program needn't handle non-finite values.
Results may differ from a plain program's by a relative error of at most 0.0035.
Values may be sent and summed in bfloat16 or wider, within the bound.
A program may use at most 192 MiB of HBM per device.

v0:
```python
import jax
import jax.numpy as jnp
from jax import lax
from jax.sharding import PartitionSpec as P

BLK = 64
KW = 4
ITERS = 2
YB = 128
XB = 128


primal_step = 0.4
first_step = 1.0
dual_step = 0.4


def from_behind(value, axis, by):
    devices = lax.axis_size(axis)
    pairs = [(i, i + by) for i in range(devices) if 0 <= i + by < devices]
    return lax.ppermute(value, axis, pairs)


def apply_blocks(block_mats, stacked):
    return jnp.einsum("roj,rjs->ros", block_mats, stacked, preferred_element_type=jnp.float32)


def transpose_blocks(block_mats, dual_rows):
    return jnp.einsum("roj,ros->rjs", block_mats, dual_rows, preferred_element_type=jnp.float32)


def one_hot_rows(indices, count):
    return (indices[None, :] == jnp.arange(count, dtype=jnp.int32)[:, None]).astype(jnp.float32)


def sum_into(selector, terms):
    return jnp.einsum(
        "bk,kos->bos",
        selector,
        terms,
        precision=lax.Precision.HIGHEST,
        preferred_element_type=jnp.float32,
    )


def body(
    coupling,
    tie_blocks,
    w_pattern,
    link_pattern,
    left_bounds,
    right_bounds,
    block_counts,
    commit_cost,
    dispatch_cost,
    demand,
    wind_error,
    commit_start,
    dispatch_start,
    dual_start,
    tie_start,
):
    row_count = coupling.shape[0]
    scen_dev = dispatch_start.shape[2]
    scen_total = scen_dev * lax.axis_size("scen")
    lead = KW * BLK
    live_tie = (lax.axis_index("net") < lax.axis_size("net") - 1).astype(jnp.float32)
    active = (jnp.arange(row_count) < block_counts[0]).astype(jnp.float32)[:, None, None]
    pattern_select = one_hot_rows(w_pattern.reshape(-1), YB)
    link_select = one_hot_rows(link_pattern, XB)
    right_select = one_hot_rows(right_bounds, YB)
    left_select = one_hot_rows(left_bounds, YB)
    recourse = coupling[:, :, :lead]
    linking = coupling[:, :, lead:]
    cost_col = dispatch_cost[:, :, None]
    target = demand[:, :, None] + wind_error.astype(jnp.float32)
    first_now = commit_start
    second_now = dispatch_start
    dual_now = dual_start * active
    tie_now = tie_start * live_tie
    for iteration in range(ITERS):
        dual_half = dual_now.astype(jnp.bfloat16)
        tie_half = tie_now.astype(jnp.bfloat16)
        recourse_terms = transpose_blocks(recourse, dual_half).reshape(
            row_count * KW, BLK, scen_dev
        )
        grad_second = sum_into(pattern_select, recourse_terms)
        link_terms = (
            jnp.einsum("roj,ros->rj", linking, dual_half, preferred_element_type=jnp.float32)
            / scen_total
        )
        grad_part = jnp.dot(
            link_select,
            link_terms,
            precision=lax.Precision.HIGHEST,
            preferred_element_type=jnp.float32,
        )
        tie_terms = transpose_blocks(tie_blocks, tie_half)
        own_terms = tie_terms[:, :BLK]
        left_terms = from_behind(tie_terms[:, BLK:], "net", 1)
        grad_second = grad_second + sum_into(right_select, own_terms)
        grad_second = grad_second + sum_into(left_select, left_terms)
        grad_first = lax.psum(grad_part.astype(jnp.bfloat16), "scen").astype(jnp.float32)
        first_next = jnp.clip(first_now - first_step * (commit_cost - grad_first), 0.0, 1.0)
        second_next = jnp.maximum(second_now - primal_step * (cost_col - grad_second), 0.0)
        first_bar = (2.0 * first_next - first_now).astype(jnp.bfloat16)
        second_bar = (2.0 * second_next - second_now).astype(jnp.bfloat16)
        next_rows = from_behind(second_bar[left_bounds], "net", -1)
        tie_inputs = jnp.concatenate([second_bar[right_bounds], next_rows], axis=1)
        tie_rows = apply_blocks(tie_blocks, tie_inputs)
        gathered = second_bar[w_pattern].reshape(row_count, lead, scen_dev)
        linked = jnp.einsum(
            "roi,ri->ro", linking, first_bar[link_pattern], preferred_element_type=jnp.float32
        )
        coupled = apply_blocks(recourse, gathered) + linked[:, :, None]
        dual_now = (dual_now + dual_step * (target - coupled)) * active
        tie_now = (tie_now - dual_step * tie_rows) * live_tie
        first_now = first_next
        second_now = second_next
    return (first_now, second_now, dual_now, tie_now)


def solution(mesh):
    return jax.shard_map(
        body,
        mesh=mesh,
        in_specs=(
            P("net", None, None),
            P("net", None, None),
            P("net", None),
            P("net"),
            P("net"),
            P("net"),
            P("net"),
            P("net", None),
            P("net", None),
            P("net", None),
            P("net", None, "scen"),
            P("net", None),
            P("net", None, "scen"),
            P("net", None, "scen"),
            P("net", None, "scen"),
        ),
        out_specs=(
            P("net", None),
            P("net", None, "scen"),
            P("net", None, "scen"),
            P("net", None, "scen"),
        ),
        check_vma=False,
    )
```

profile of v0, /device:TPU:0, one launch (start us, length us, event | category | flops | bytes accessed | tf_op | source)
XLA Modules:
  0.0 271.5 jit_solution(8567158418583271729)
XLA Ops:
  0.6 0.0 copy-start
  0.7 1.6 copy-done
  2.2 3.7 %convolution_bitcast_fusion.3 = f32[128,128,128]{2,1,0:T(8,128)S(1)} fusion(bf16[128,64,128]{2,1,0:T(8,128)(2,1)S(1)} %copy-done, f32[128,64,128]{2,1,0:T(8,128)} %param.29, f32[]{:T(128)S(6)} %convert_element_type.65), kind=kOutput, calls=%fused_computation.40 | convolution fusion | flops 270532608 | bytes 14680068 | tf_op jit(solution)/shard_map/roj,ros->rjs/dot_general | solution.py:29
  5.9 0.0 slice-start.1
  5.9 0.0 copy-start.5
  5.9 4.3 %fusion.85 = (f32[128,64,128]{2,1,0:T(8,128)}, f32[128,64,128]{2,1,0:T(8,128)}) fusion(f32[128,128,128]{2,1,0:T(8,128)S(1)} %convolution_bitcast_fusion.3), kind=kLoop, calls=%fused_computation.111 | loop fusion | bytes 16777216 | tf_op jit(solution)/shard_map/slice | solution.py:100
  10.2 4.3 %collective-permute-start = (f32[128,64,128]{2,1,0:T(8,128)}, f32[128,64,128]{2,1,0:T(8,128)}, u32[]{:S(2)}, u32[]{:S(2)}) collective-permute-start(f32[128,64,128]{2,1,0:T(8,128)} %get-tuple-element.16), channel_id=1, source_target_pairs={{0,1},{1,2},{2,3},{3,4},{4,5},{5,6},{6,7},{8,9},{9,10},{10,11},{11... | collective-permute-start | bytes 12582920 | tf_op jit(solution)/shard_map/ppermute | solution.py:21
  15.2 6.9 %convolution_bitcast_fusion.1 = f32[96,256,128]{1,2,0:T(8,128)} fusion(bf16[96,64,320]{2,1,0:T(8,128)(2,1)S(1)} %bitcast.81, f32[96,64,128]{2,1,0:T(8,128)S(1)} %copy-done.5, f32[96]{0:T(128)S(1)} %compare_convert_fusion), kind=kOutput, calls=%fused_computation.13 | convolution fusion | flops 404226048 | bytes 18874880 | tf_op jit(solution)/shard_map/roj,ros->rjs/dot_general | solution.py:29
  22.1 12.8 %copy.33 = f32[96,256,128]{2,1,0:T(8,128)} copy(f32[96,256,128]{1,2,0:T(8,128)} %convolution_bitcast_fusion.1) | data formatting | bytes 25165824 | tf_op jit(solution)/shard_map/roj,ros->rjs/dot_general | solution.py:29
  35.0 0.1 copy.32
  35.1 0.1 eq.57
  35.2 6.7 %fusion.20 = f32[128,64,128]{2,0,1:T(8,128)S(1)} fusion(f32[128,64,128]{2,1,0:T(8,128)} %get-tuple-element.17, s32[128]{0:T(128)S(1)} %copy-done.16), kind=kOutput, calls=%fused_computation.32 | convolution fusion | flops 1610629120 | bytes 8389120 | tf_op jit(solution)/shard_map/bk,kos->bos/dot_general | solution.py:37
  41.9 0.0 copy-start.9
  41.9 0.0 copy-start.10
  41.9 16.6 %fusion.2 = f32[128,64,128]{2,0,1:T(8,128)S(1)} fusion(f32[384,64,128]{2,1,0:T(8,128)} %bitcast.78, s32[384]{0:T(512)S(1)} %eq.57), kind=kOutput, calls=%fused_computation.10 | convolution fusion | flops 4831887360 | bytes 16778752 | tf_op jit(solution)/shard_map/bk,kos->bos/dot_general | solution.py:37
  58.6 13.5 %subtract_convert_fusion.1 = (bf16[128,64,128]{2,0,1:T(8,128)(2,1)S(1)}, f32[128,64,128]{2,0,1:T(8,128)}) fusion(f32[128,64,128]{2,1,0:T(8,128)S(1)} %copy-done.9, f32[128,64,128]{2,1,0:T(8,128)} %collective-permute-done, s32[128]{0:T(128)S(1)} %copy-done.15, f32[128,64,128]{2,0,1:T(8,128)S(1)} %fusion.2, f32[128,64,128]{2,0,1:T(8,128)S(1)} %fusion.20, ...), kind=kOutput, calls=%fused_computation.36 | convolution fusion | flops 1620066304 | bytes 23101952 | tf_op jit(solution)/shard_map/bk,kos->bos/dot_general | solution.py:37
  72.1 2.7 copy.40
  74.7 3.7 %gather_fusion.3 = bf16[128,64,128]{2,1,0:T(8,128)(2,1)} fusion(bf16[128,64,128]{2,1,0:T(8,128)(2,1)} %copy.40, s32[1024]{0:T(1024)S(1)} %pad_clamp_fusion), kind=kCustom, calls=%fused_computation.3 | custom fusion | bytes 4194816 | tf_op jit(solution)/shard_map/gather | solution.py:108
  78.5 1.3 collective-permute-start.1
  79.8 2.9 %convert_reduce_fusion.1 = f32[96,64]{1,0:T(8,128)S(1)} fusion(f32[96,64,128]{2,1,0:T(8,128)} %param.28, f32[96]{0:T(128)S(1)} %compare_convert_fusion), kind=kLoop, calls=%fused_computation.51 | loop fusion | flops 3139584 | bytes 3170688 | tf_op jit(solution)/shard_map/roj,ros->rj/reduce_sum | solution.py:89
  82.7 3.7 %gather_fusion.2 = bf16[128,64,128]{2,1,0:T(8,128)(2,1)} fusion(bf16[128,64,128]{2,1,0:T(8,128)(2,1)} %copy.40, s32[1024]{0:T(1024)S(1)} %pad_clamp_fusion.1), kind=kCustom, calls=%fused_computation.2 | custom fusion | bytes 4194816 | tf_op jit(solution)/shard_map/gather | solution.py:109
  86.4 0.3 collective-permute-done.1
  86.7 4.7 %fusion.13 = f32[128,64,128]{2,1,0:T(8,128)S(1)} fusion(f32[128,64,128]{2,1,0:T(8,128)} %param.29, bf16[128,64,128]{2,1,0:T(8,128)(2,1)S(1)} %copy-done, bf16[128,64,128]{2,1,0:T(8,128)(2,1)} %collective-permute-done.1, bf16[128,64,128]{2,1,0:T(8,128)(2,1)} %gather_fusion.2, f32[]{:T(128)S(6)} %convert_element_type.65), kind=kOutput, calls=%fused_computation.25 | convolution fusion | flops 281018368 | bytes 14680068 | tf_op jit(solution)/shard_map/roj,rjs->ros/dot_general | solution.py:25
  91.4 2.0 copy-done.1
  93.3 1.3 convolution_bitcast_fusion.2
  94.7 0.0 copy-start.17
  94.7 0.0 copy-start.11
  94.7 0.0 copy-start.12
  94.7 0.0 copy-start.13
  94.7 4.2 %fusion.84 = (f32[128,64,128]{2,1,0:T(8,128)}, f32[128,64,128]{2,1,0:T(8,128)}) fusion(f32[128,128,128]{2,1,0:T(8,128)S(1)} %convolution_bitcast_fusion.2), kind=kLoop, calls=%fused_computation.110 | loop fusion | bytes 16777216 | tf_op jit(solution)/shard_map/slice | solution.py:100
  98.9 26.5 %collective-permute-start.2 = (f32[128,64,128]{2,1,0:T(8,128)}, f32[128,64,128]{2,1,0:T(8,128)}, u32[]{:S(2)}, u32[]{:S(2)}) collective-permute-start(f32[128,64,128]{2,1,0:T(8,128)} %get-tuple-element.14), channel_id=1, source_target_pairs={{0,1},{1,2},{2,3},{3,4},{4,5},{5,6},{6,7},{8,9},{9,10},{10,11},{11... | collective-permute-start | bytes 12582920 | tf_op jit(solution)/shard_map/ppermute | solution.py:21
  125.4 1.9 fusion.54
  127.4 0.2 convolution_convert_fusion.1
  127.6 19.2 %psum.14 = bf16[128,64]{0,1:T(8,128)(2,1)S(1)} all-reduce(bf16[128,64]{0,1:T(8,128)(2,1)S(1)} %convolution_convert_fusion.1), channel_id=1, replica_groups=mesh['scen'=4,'net'=8] {'scen'}, use_global_device_ids=true, to_apply=%region_1.0 | all-reduce | flops 8192 | bytes 32768 | tf_op jit(solution)/shard_map/psum | solution.py:103
  146.9 0.1 copy.41
  147.0 0.1 copy.39
  147.1 0.1 reshape.39
  147.2 0.1 copy.31
  147.4 0.7 gather_fusion.1
  148.0 2.3 fusion.52
  150.4 5.7 %gather_fusion = bf16[384,64,128]{2,1,0:T(8,128)(2,1)} fusion(bf16[128,64,128]{2,1,0:T(8,128)(2,1)} %copy.40, s32[1024]{0:T(1024)S(1)} %pad_clamp_fusion.3), kind=kCustom, calls=%fused_computation | custom fusion | bytes 12584448 | tf_op jit(solution)/shard_map/gather | solution.py:111
  156.0 6.8 %convert_reduce_fusion = (f32[96,64]{1,0:T(8,128)S(1)}, f32[96,64,128]{2,1,0:T(8,128)S(1)}) fusion(f32[96,64]{1,0:T(8,128)S(1)} %bitcast.93, bf16[96,256,128]{2,1,0:T(8,128)(2,1)} %bitcast.87, bf16[96,64,320]{2,1,0:T(8,128)(2,1)} %param.15, bf16[96,64,128]{2,1,0:T(8,128)(2,1)} %param.25, f32[96,64]{1,0:T(8,128)S(1)} %copy.31, f32[96,64,128]{2,1,0:T(8,128)} %param.28, ...), kind=kOutput, calls=%fused_computation.49 | convolution fusion | flops 411297792 | bytes 17375616 | tf_op jit(solution)/shard_map/roj,rjs->ros/dot_general | solution.py:25
  162.8 1.7 copy-done.3
  164.5 6.4 %convolution_bitcast_fusion = f32[96,256,128]{1,2,0:T(8,128)} fusion(bf16[96,64,320]{2,1,0:T(8,128)(2,1)S(1)} %bitcast.83, f32[96,64,128]{2,1,0:T(8,128)S(1)} %get-tuple-element.21), kind=kOutput, calls=%fused_computation.12 | convolution fusion | flops 403439616 | bytes 18874368 | tf_op jit(solution)/shard_map/roj,ros->rjs/dot_general | solution.py:29
  170.9 12.6 %copy.42 = f32[96,256,128]{2,1,0:T(8,128)} copy(f32[96,256,128]{1,2,0:T(8,128)} %convolution_bitcast_fusion) | data formatting | bytes 25165824 | tf_op jit(solution)/shard_map/roj,ros->rjs/dot_general | solution.py:29
  183.5 16.6 %fusion = f32[128,64,128]{2,0,1:T(8,128)S(1)} fusion(f32[384,64,128]{2,1,0:T(8,128)} %bitcast.79, s32[384]{0:T(512)S(1)} %eq.57), kind=kOutput, calls=%fused_computation.8 | convolution fusion | flops 4831887360 | bytes 16778752 | tf_op jit(solution)/shard_map/bk,kos->bos/dot_general | solution.py:37
  200.1 4.7 %fusion.16 = f32[128,64,128]{2,0,1:T(8,128)S(1)} fusion(f32[128,64,128]{2,1,0:T(8,128)S(1)} %copy-done.7, s32[128]{0:T(128)S(1)} %copy-done.16), kind=kOutput, calls=%fused_computation.28 | convolution fusion | flops 1610629120 | bytes 8389120 | tf_op jit(solution)/shard_map/bk,kos->bos/dot_general | solution.py:37
  204.8 9.8 %subtract_convert_fusion = (bf16[128,64,128]{2,0,1:T(8,128)(2,1)S(1)}, f32[128,64,128]{2,0,1:T(8,128)}) fusion(f32[128,64,128]{2,0,1:T(8,128)S(1)} %copy-done.6, f32[128,64,128]{2,1,0:T(8,128)} %collective-permute-done.2, s32[128]{0:T(128)S(1)} %copy-done.15, f32[128,64,128]{2,0,1:T(8,128)S(1)} %fusion, f32[128,64,128]{2,0,1:T(8,128)S(1)} %fusion.16, ...), kind=kOutput, calls=%fused_computation.34 | convolution fusion | flops 1620066304 | bytes 23101952 | tf_op jit(solution)/shard_map/bk,kos->bos/dot_general | solution.py:37
  214.6 2.7 copy.48
  217.3 3.8 %gather_fusion.7 = bf16[128,64,128]{2,1,0:T(8,128)(2,1)} fusion(bf16[128,64,128]{2,1,0:T(8,128)(2,1)} %copy.48, s32[1024]{0:T(1024)S(1)} %pad_clamp_fusion), kind=kCustom, calls=%fused_computation.7 | custom fusion | bytes 4194816 | tf_op jit(solution)/shard_map/gather | solution.py:108
  221.1 1.3 collective-permute-start.3
  222.4 1.9 fusion.50
  224.3 0.2 convolution_convert_fusion
  224.6 15.5 %psum.15 = bf16[128,64]{0,1:T(8,128)(2,1)S(1)} all-reduce(bf16[128,64]{0,1:T(8,128)(2,1)S(1)} %convolution_convert_fusion), channel_id=1, replica_groups=mesh['scen'=4,'net'=8] {'scen'}, use_global_device_ids=true, to_apply=%region_3.4 | all-reduce | flops 8192 | bytes 32768 | tf_op jit(solution)/shard_map/psum | solution.py:103
  240.1 0.6 subtract_convert_fusion.2
  240.7 0.1 copy.49
  240.8 0.7 gather_fusion.5
  241.5 2.3 fusion.48
  243.8 5.6 %gather_fusion.4 = bf16[384,64,128]{2,1,0:T(8,128)(2,1)} fusion(bf16[128,64,128]{2,1,0:T(8,128)(2,1)} %copy.48, s32[1024]{0:T(1024)S(1)} %pad_clamp_fusion.3), kind=kCustom, calls=%fused_computation.4 | custom fusion | bytes 12584448 | tf_op jit(solution)/shard_map/gather | solution.py:111
  249.5 3.8 %gather_fusion.6 = bf16[128,64,128]{2,1,0:T(8,128)(2,1)} fusion(bf16[128,64,128]{2,1,0:T(8,128)(2,1)} %copy.48, s32[1024]{0:T(1024)S(1)} %pad_clamp_fusion.1), kind=kCustom, calls=%fused_computation.6 | custom fusion | bytes 4194816 | tf_op jit(solution)/shard_map/gather | solution.py:109
  253.3 6.8 %copy.52 = f32[128,64,128]{2,1,0:T(8,128)} copy(f32[128,64,128]{2,0,1:T(8,128)} %get-tuple-element.23) | data formatting | bytes 8388608
  260.1 5.5 %fusion.24 = f32[96,64,128]{2,1,0:T(8,128)} fusion(f32[96,64,128]{2,1,0:T(8,128)S(1)} %copy-done.4, bf16[96,64,128]{2,1,0:T(8,128)(2,1)} %param.25, bf16[96,256,128]{2,1,0:T(8,128)(2,1)} %bitcast.86, bf16[96,64,320]{2,1,0:T(8,128)(2,1)S(1)} %bitcast.85, f32[96,64]{1,0:T(8,128)S(1)} %bitcast.88, f32[96,64]{1,0:T(8,128)S(1)} %copy.31, ...), kind=kOutput, calls=%fused_computation.44 | convolution fusion | flops 408158208 | bytes 17400320 | tf_op jit(solution)/shard_map/roj,rjs->ros/dot_general | solution.py:25
  265.7 0.7 copy-done.8
  266.4 4.9 %fusion.12 = f32[128,64,128]{2,1,0:T(8,128)} fusion(f32[128,64,128]{2,1,0:T(8,128)S(1)} %copy-done.2, bf16[128,64,128]{2,1,0:T(8,128)(2,1)S(1)} %copy-done, bf16[128,64,128]{2,1,0:T(8,128)(2,1)} %collective-permute-done.3, bf16[128,64,128]{2,1,0:T(8,128)(2,1)S(1)} %copy-done.8, f32[]{:T(128)S(6)} %convert_element_type.65), kind=kOutput, calls=%fused_computation.23 | convolution fusion | flops 279969792 | bytes 14680068 | tf_op jit(solution)/shard_map/roj,rjs->ros/dot_general | solution.py:25
  (51 shorter events, 0.1 us)
Async XLA Ops:
  0.6 1.6 copy-start
  2.2 13.0 %slice-start = ((s8[4718592]{0:T(1024)(128)(4,1)}), s8[4194304]{0:T(1024)(128)(4,1)S(1)}, s32[]{:S(2)}) async-start(s8[4718592]{0:T(1024)(128)(4,1)} %bitcast.80), calls=%async_computation | async-start | bytes 8388608
  5.9 9.3 %slice-start.1 = ((s8[4718592]{0:T(1024)(128)(4,1)}), s8[524288]{0:T(1024)(128)(4,1)S(1)}, s32[]{:S(2)}) async-start(s8[4718592]{0:T(1024)(128)(4,1)} %bitcast.80), calls=%async_computation.1 | async-start | bytes 1048576
  5.9 9.3 %copy-start.5 = (f32[96,64,128]{2,1,0:T(8,128)S(1)}, f32[96,64,128]{2,1,0:T(8,128)}, u32[]{:S(2)}) copy-start(f32[96,64,128]{2,1,0:T(8,128)} %param.28) | copy-start | bytes 9437188
  10.2 48.3 %collective-permute-start = (f32[128,64,128]{2,1,0:T(8,128)}, f32[128,64,128]{2,1,0:T(8,128)}, u32[]{:S(2)}, u32[]{:S(2)}) collective-permute-start(f32[128,64,128]{2,1,0:T(8,128)} %get-tuple-element.16), channel_id=1, source_target_pairs={{0,1},{1,2},{2,3},{3,4},{4,5},{5,6},{6,7},{8,9},{9,10},{10,11},{11... | collective-permute-start | bytes 12582920 | tf_op jit(solution)/shard_map/ppermute | solution.py:21
  22.1 12.8 %copy-start.14 = (s32[96,4]{0,1:T(4,128)S(1)}, s32[96,4]{0,1:T(4,128)}, u32[]{:S(2)}) copy-start(s32[96,4]{0,1:T(4,128)} %param.17) | copy-start | bytes 4612
  22.1 13.0 %copy-start.15 = (s32[128]{0:T(128)S(1)}, s32[128]{0:T(128)}, u32[]{:S(2)}) copy-start(s32[128]{0:T(128)} %param.19) | copy-start | bytes 1540
  22.1 13.1 %copy-start.16 = (s32[128]{0:T(128)S(1)}, s32[128]{0:T(128)}, u32[]{:S(2)}) copy-start(s32[128]{0:T(128)} %param.20) | copy-start | bytes 1540
  41.9 16.7 %copy-start.9 = (f32[128,64,128]{2,1,0:T(8,128)S(1)}, f32[128,64,128]{2,1,0:T(8,128)}, u32[]{:S(2)}) copy-start(f32[128,64,128]{2,1,0:T(8,128)} %param.27) | copy-start | bytes 12582916
  41.9 16.7 %copy-start.10 = (f32[128,64]{0,1:T(8,128)S(1)}, f32[128,64]{0,1:T(8,128)}, u32[]{:S(2)}) copy-start(f32[128,64]{0,1:T(8,128)} %param.23) | copy-start | bytes 98308
  78.5 8.2 %collective-permute-start.1 = (bf16[128,64,128]{2,1,0:T(8,128)(2,1)}, bf16[128,64,128]{2,1,0:T(8,128)(2,1)}, u32[]{:S(2)}, u32[]{:S(2)}) collective-permute-start(bf16[128,64,128]{2,1,0:T(8,128)(2,1)} %gather_fusion.3), channel_id=1, source_target_pairs={{1,0},{2,1},{3,2},{4,3},{5,4},{6,5},{7,6},{9,8},{10,9},{11,10},{12... | collective-permute-start | bytes 6291464 | tf_op jit(solution)/shard_map/ppermute | solution.py:21
  91.4 2.0 copy-start.1
  94.7 32.7 %copy-start.17 = (s32[96]{0:T(128)S(1)}, s32[96]{0:T(128)}, u32[]{:S(2)}) copy-start(s32[96]{0:T(128)} %param.18) | copy-start | bytes 1156
  94.7 52.2 %copy-start.11 = (f32[128,64]{0,1:T(8,128)S(1)}, f32[128,64]{0,1:T(8,128)}, u32[]{:S(2)}) copy-start(f32[128,64]{0,1:T(8,128)} %param.26) | copy-start | bytes 98308
  94.7 52.2 %copy-start.12 = (f32[128,64]{0,1:T(8,128)S(1)}, f32[128,64]{0,1:T(8,128)}, u32[]{:S(2)}) copy-start(f32[128,64]{0,1:T(8,128)} %param.22) | copy-start | bytes 98308
  94.7 52.5 %copy-start.13 = (f32[96,64]{0,1:T(8,128)S(1)}, f32[96,64]{0,1:T(8,128)}, u32[]{:S(2)}) copy-start(f32[96,64]{0,1:T(8,128)} %param.24) | copy-start | bytes 73732
  98.9 105.9 %collective-permute-start.2 = (f32[128,64,128]{2,1,0:T(8,128)}, f32[128,64,128]{2,1,0:T(8,128)}, u32[]{:S(2)}, u32[]{:S(2)}) collective-permute-start(f32[128,64,128]{2,1,0:T(8,128)} %get-tuple-element.14), channel_id=1, source_target_pairs={{0,1},{1,2},{2,3},{3,4},{4,5},{5,6},{6,7},{8,9},{9,10},{10,11},{11... | collective-permute-start | bytes 12582920 | tf_op jit(solution)/shard_map/ppermute | solution.py:21
  150.3 14.1 %slice-start.2 = ((s8[4718592]{0:T(1024)(128)(4,1)}), s8[524288]{0:T(1024)(128)(4,1)S(1)}, s32[]{:S(2)}) async-start(s8[4718592]{0:T(1024)(128)(4,1)} %bitcast.82), calls=%async_computation.2 | async-start | bytes 1048576
  156.0 8.4 %slice-start.3 = ((s8[4718592]{0:T(1024)(128)(4,1)}), s8[4194304]{0:T(1024)(128)(4,1)S(1)}, s32[]{:S(2)}) async-start(s8[4718592]{0:T(1024)(128)(4,1)} %bitcast.82), calls=%async_computation.3 | async-start | bytes 8388608
  162.8 1.7 copy-start.3
  183.5 16.6 %copy-start.7 = (f32[128,64,128]{2,1,0:T(8,128)S(1)}, f32[128,64,128]{2,1,0:T(8,128)}, u32[]{:S(2)}) copy-start(f32[128,64,128]{2,1,0:T(8,128)} %get-tuple-element.15) | copy-start | bytes 12582916
  200.1 4.7 %copy-start.6 = (f32[128,64,128]{2,0,1:T(8,128)S(1)}, f32[128,64,128]{2,0,1:T(8,128)}, u32[]{:S(2)}) copy-start(f32[128,64,128]{2,0,1:T(8,128)} %get-tuple-element.19) | copy-start | bytes 12582916
  221.1 44.5 %collective-permute-start.3 = (bf16[128,64,128]{2,1,0:T(8,128)(2,1)}, bf16[128,64,128]{2,1,0:T(8,128)(2,1)}, u32[]{:S(2)}, u32[]{:S(2)}) collective-permute-start(bf16[128,64,128]{2,1,0:T(8,128)(2,1)} %gather_fusion.7), channel_id=1, source_target_pairs={{1,0},{2,1},{3,2},{4,3},{5,4},{6,5},{7,6},{9,8},{10,9},{11,10},{12... | collective-permute-start | bytes 6291464 | tf_op jit(solution)/shard_map/ppermute | solution.py:21
  249.5 10.6 %slice-start.4 = ((s8[4718592]{0:T(1024)(128)(4,1)}), s8[524288]{0:T(1024)(128)(4,1)S(1)}, s32[]{:S(2)}) async-start(s8[4718592]{0:T(1024)(128)(4,1)} %bitcast.84), calls=%async_computation.4 | async-start | bytes 1048576
  253.3 6.8 %slice-start.5 = ((s8[4718592]{0:T(1024)(128)(4,1)}), s8[4194304]{0:T(1024)(128)(4,1)S(1)}, s32[]{:S(2)}) async-start(s8[4718592]{0:T(1024)(128)(4,1)} %bitcast.84), calls=%async_computation.5 | async-start | bytes 8388608
  253.3 6.8 %copy-start.4 = (f32[96,64,128]{2,1,0:T(8,128)S(1)}, f32[96,64,128]{2,1,0:T(8,128)}, u32[]{:S(2)}) copy-start(f32[96,64,128]{2,1,0:T(8,128)} %copy-done.3) | copy-start | bytes 9437188
  260.1 5.6 %copy-start.2 = (f32[128,64,128]{2,1,0:T(8,128)S(1)}, f32[128,64,128]{2,1,0:T(8,128)}, u32[]{:S(2)}) copy-start(f32[128,64,128]{2,1,0:T(8,128)} %copy-done.1) | copy-start | bytes 12582916
  260.1 6.3 %copy-start.8 = (bf16[128,64,128]{2,1,0:T(8,128)(2,1)S(1)}, bf16[128,64,128]{2,1,0:T(8,128)(2,1)}, u32[]{:S(2)}) copy-start(bf16[128,64,128]{2,1,0:T(8,128)(2,1)} %gather_fusion.6) | copy-start | bytes 6291460
where the time goes:
time: 276 us; the launch traced here: 272 us
  matrix products  117 us (42%)
  local copies, waits for them, and re-layouts  80.6 us (29%)
  blocking collectives  34.8 us (13%)
  starting transfers between devices  33.4 us (12%)
  other arithmetic  3.58 us (1%)
    dot_general x6, matrix products, sum_into(): jnp.einsum('bk,kos->bos', selector, terms, precision=lax.Precision.HIGHES...  67.9 us
    psum x2, blocking collectives, body(): lax.psum(grad_part.astype(jnp.bfloat16), 'scen').astype(jnp.float32)  34.8 us
    ppermute x4, starting transfers between devices, from_behind(): return lax.ppermute(value, axis, pairs)  33.4 us
    dot_general x2, local copies, waits for them, and re-layouts, transpose_blocks(): jnp.einsum('roj,ros->rjs', block_mats, dual_rows, preferred_element_type=...  25.5 us
    dot_general x4, matrix products, apply_blocks(): jnp.einsum('roj,rjs->ros', block_mats, stacked, preferred_element_type=jn...  21.9 us
    dot_general x4, matrix products, transpose_blocks(): jnp.einsum('roj,ros->rjs', block_mats, dual_rows, preferred_element_type=...  18.3 us
    unnamed x51, local copies, waits for them, and re-layouts  13 us
    gather x2, local copies, waits for them, and re-layouts, body(): gathered = second_bar[w_pattern].reshape(row_count, lead, scen_dev)  11.3 us
  transfers between devices with their start and end apart: 4, of which 1 were waited for; matrix products, arithmetic and copies ran while one was open for 50% of the time, Pallas kernels for 0%

commit v1 on v0

v1 whole, which is shorter than its diff:
```python
import jax
import jax.numpy as jnp
from jax import lax
from jax.experimental import pallas as pl
from jax.experimental.pallas import tpu as pltpu
from jax.sharding import PartitionSpec as P

BLK = 64
KW = 4
ITERS = 2
UNROLL = 4

primal_step = 0.4
first_step = 1.0
dual_step = 0.4

VMEM = pl.BlockSpec(memory_space=pltpu.VMEM)
SMEM = pl.BlockSpec(memory_space=pltpu.SMEM)
F32 = jnp.float32
BF16 = jnp.bfloat16


def from_behind(value, axis, by):
    devices = lax.axis_size(axis)
    pairs = [(i, i + by) for i in range(devices) if 0 <= i + by < devices]
    return lax.ppermute(value, axis, pairs)


def local_call(kernel, out_shape, in_specs, flops, moved):
    return pl.pallas_call(
        kernel,
        out_shape=out_shape,
        in_specs=in_specs,
        out_specs=jax.tree.map(lambda _: VMEM, out_shape),
        compiler_params=pltpu.CompilerParams(vmem_limit_bytes=48 * 2**20),
        cost_estimate=pl.CostEstimate(flops=flops, bytes_accessed=moved, transcendentals=0),
    )


def rows_loop(count, step):
    def chunk(c, carry):
        step([c * UNROLL + u for u in range(UNROLL)])
        return carry

    lax.fori_loop(0, count // UNROLL, chunk, 0)


def transposed_dot(a, b):
    return lax.dot_general(a, b, (((0,), (0,)), ((), ())), preferred_element_type=F32)


def left_terms_kernel(live, tie, mu, terms):
    def step(rows):
        for j in rows:
            half = (mu[j] * live[0]).astype(BF16)
            terms[j] = transposed_dot(tie[j], half)[BLK:].astype(BF16)

    rows_loop(tie.shape[0], step)


def gradient_kernel(live, count, pattern, link, right, coupling, tie, lam, mu, grad, grad_first):
    grad[...] = jnp.zeros_like(grad)
    grad_first[...] = jnp.zeros_like(grad_first)
    ones = jnp.ones((8, lam.shape[2]), BF16)

    def tie_step(rows):
        parts = [transposed_dot(tie[j], (mu[j] * live[0]).astype(BF16))[:BLK] for j in rows]
        for j, part in zip(rows, parts):
            grad[right[j]] += part

    rows_loop(tie.shape[0], tie_step)

    def row_step(rows):
        halves = [jnp.where(r < count[0], lam[r], 0.0).astype(BF16) for r in rows]
        parts = [transposed_dot(coupling[r, :, : KW * BLK], h) for r, h in zip(rows, halves)]
        firsts = []
        for r, h in zip(rows, halves):
            total = lax.dot_general(ones, h, (((1,), (1,)), ((), ())), preferred_element_type=F32)
            firsts.append(
                lax.dot_general(
                    total,
                    coupling[r, :, KW * BLK :].astype(F32),
                    (((1,), (0,)), ((), ())),
                    precision=lax.Precision.HIGHEST,
                    preferred_element_type=F32,
                )
            )
        for r, part, first in zip(rows, parts, firsts):
            for k in range(KW):
                grad[pattern[r * KW + k]] += part[k * BLK : (k + 1) * BLK]
            grad_first[pl.ds(link[r], 1), :] += first[:1]

    rows_loop(coupling.shape[0], row_step)


def primal_kernel(left, received, grad, cost, second, next_left, second_next, second_bar, sent, total):
    total[...] = grad[...]

    def add_step(rows):
        for j in rows:
            total[left[j]] += received[j].astype(F32)

    rows_loop(received.shape[0], add_step)

    def move_step(rows):
        for b in rows:
            now = second[b]
            new = jnp.maximum(now - primal_step * (cost[b] - total[b]), 0.0)
            second_next[b] = new
            second_bar[b] = (2.0 * new - now).astype(BF16)

    rows_loop(second.shape[0], move_step)

    def gather_step(rows):
        for j in rows:
            sent[j] = second_bar[left[j]]

    rows_loop(received.shape[0], gather_step)


def dual_kernel(live, count, pattern, link, right, coupling, tie, bar, first, target, lam, mu, lam_next, mu_part):
    def row_step(rows):
        for r in rows:
            gathered = [bar[pattern[r * KW + k]] for k in range(KW)] + [first[link[r]]]
            coupled = jnp.dot(coupling[r], jnp.concatenate(gathered, axis=0), preferred_element_type=F32)
            new = lam[r] + dual_step * (target[r] - coupled)
            lam_next[r] = jnp.where(r < count[0], new, 0.0)

    rows_loop(coupling.shape[0], row_step)

    def tie_step(rows):
        for j in rows:
            own = jnp.dot(tie[j, :, :BLK], bar[right[j]], preferred_element_type=F32)
            mu_part[j] = mu[j] * live[0] - dual_step * own

    rows_loop(tie.shape[0], tie_step)


def tie_kernel(live, tie, mu_part, arrived, mu_next, *terms):
    def step(rows):
        for j in rows:
            block = tie[j]
            new = (
                mu_part[j]
                - dual_step * jnp.dot(block[:, BLK:], arrived[j], preferred_element_type=F32)
            ) * live[0]
            mu_next[j] = new
            if terms:
                terms[0][j] = transposed_dot(block, new.astype(BF16))[BLK:].astype(BF16)

    rows_loop(tie.shape[0], step)


def primal_call(left, received, grad, cost, second):
    shape = second.shape

    def kernel(left, received, grad, cost, second, second_next, second_bar, sent, total):
        primal_kernel(left, received, grad, cost, second, None, second_next, second_bar, sent, total)

    return pl.pallas_call(
        kernel,
        out_shape=(
            jax.ShapeDtypeStruct(shape, F32),
            jax.ShapeDtypeStruct(shape, BF16),
            jax.ShapeDtypeStruct(received.shape, BF16),
        ),
        in_specs=[SMEM] + [VMEM] * 4,
        out_specs=(VMEM,) * 3,
        scratch_shapes=[pltpu.VMEM(shape, F32)],
        compiler_params=pltpu.CompilerParams(vmem_limit_bytes=48 * 2**20),
        cost_estimate=pl.CostEstimate(flops=10**7, bytes_accessed=25 * 10**6, transcendentals=0),
    )(left, received, grad, cost, second)


def body(
    coupling,
    tie_blocks,
    w_pattern,
    link_pattern,
    left_bounds,
    right_bounds,
    block_counts,
    commit_cost,
    dispatch_cost,
    demand,
    wind_error,
    commit_start,
    dispatch_start,
    dual_start,
    tie_start,
):
    scen_dev = dispatch_start.shape[2]
    scen_total = scen_dev * lax.axis_size("scen")
    second_shape = dispatch_start.shape
    tie_shape = tie_start.shape
    live = (lax.axis_index("net") < lax.axis_size("net") - 1).astype(F32).reshape(1)
    pattern = w_pattern.reshape(-1)
    cost = jnp.broadcast_to(dispatch_cost[:, :, None], second_shape)
    target = demand[:, :, None] + wind_error.astype(F32)
    first_now = commit_start
    second_now = dispatch_start
    dual_now = dual_start
    tie_now = tie_start
    terms = local_call(
        left_terms_kernel, jax.ShapeDtypeStruct(tie_shape, BF16), [SMEM, VMEM, VMEM], 3 * 10**8, 10**7
    )(live, tie_blocks, tie_start)
    for iteration in range(ITERS):
        received = from_behind(terms, "net", 1)
        grad, grad_part = local_call(
            gradient_kernel,
            (jax.ShapeDtypeStruct(second_shape, F32), jax.ShapeDtypeStruct(first_now.shape, F32)),
            [SMEM] * 5 + [VMEM] * 4,
            8 * 10**8,
            18 * 10**6,
        )(live, block_counts, pattern, link_pattern, right_bounds, coupling, tie_blocks, dual_now, tie_now)
        grad_first = lax.psum((grad_part / scen_total).astype(BF16), "scen").astype(F32)
        first_next = jnp.clip(first_now - first_step * (commit_cost - grad_first), 0.0, 1.0)
        first_bar = (2.0 * first_next - first_now).astype(BF16)
        first_wide = jnp.broadcast_to(first_bar[:, :, None], first_bar.shape + (scen_dev,))
        second_next, second_bar, sent = primal_call(left_bounds, received, grad, cost, second_now)
        arrived = from_behind(sent, "net", -1)
        dual_now, tie_part = local_call(
            dual_kernel,
            (jax.ShapeDtypeStruct(dual_start.shape, F32), jax.ShapeDtypeStruct(tie_shape, F32)),
            [SMEM] * 5 + [VMEM] * 7,
            8 * 10**8,
            30 * 10**6,
        )(
            live, block_counts, pattern, link_pattern, right_bounds,
            coupling, tie_blocks, second_bar, first_wide, target, dual_now, tie_now,
        )
        more = iteration < ITERS - 1
        outs = (jax.ShapeDtypeStruct(tie_shape, F32),)
        if more:
            outs += (jax.ShapeDtypeStruct(tie_shape, BF16),)
        got = local_call(tie_kernel, outs, [SMEM] + [VMEM] * 3, 4 * 10**8, 15 * 10**6)(
            live, tie_blocks, tie_part, arrived
        )
        tie_now = got[0]
        if more:
            terms = got[1]
        first_now = first_next
        second_now = second_next
    return (first_now, second_now, dual_now, tie_now)


def solution(mesh):
    return jax.shard_map(
        body,
        mesh=mesh,
        in_specs=(
            P("net", None, None),
            P("net", None, None),
            P("net", None),
            P("net"),
            P("net"),
            P("net"),
            P("net"),
            P("net", None),
            P("net", None),
            P("net", None),
            P("net", None, "scen"),
            P("net", None),
            P("net", None, "scen"),
            P("net", None, "scen"),
            P("net", None, "scen"),
        ),
        out_specs=(
            P("net", None),
            P("net", None, "scen"),
            P("net", None, "scen"),
            P("net", None, "scen"),
        ),
        check_vma=False,
    )
```

time: 276 us -> 235 us (0.85)
  the two profiles are of different devices: /device:TPU:0 before, /device:TPU:1 now
where the time goes in v1:
time: 235 us; the launch traced here: 230 us
  Pallas kernels  166 us (71%)
  blocking collectives  28.1 us (12%)
  local copies, waits for them, and re-layouts  15.7 us (7%)
  starting transfers between devices  15.5 us (7%)
  other arithmetic  3.48 us (1%)
    pallas_call x2, Pallas kernels, body(): local_call(gradient_kernel, (jax.ShapeDtypeStruct(second_shape, F32), jax...  64.9 us
    pallas_call x2, Pallas kernels, body(): local_call(dual_kernel, (jax.ShapeDtypeStruct(dual_start.shape, F32), jax...  37.2 us
    pallas_call x2, Pallas kernels, body(): local_call(tie_kernel, outs, [SMEM] + [VMEM] * 3, 4 * 10 ** 8, 15 * 10 ** 6)  32.4 us
    psum x2, blocking collectives, body(): lax.psum((grad_part / scen_total).astype(BF16), 'scen').astype(F32)  28.1 us
    pallas_call x2, Pallas kernels, primal_call(): pl.pallas_call(kernel, out_shape=(jax.ShapeDtypeStruct(shape, F32), jax.S...  20.7 us
    ppermute x4, starting transfers between devices, from_behind(): return lax.ppermute(value, axis, pairs)  15.5 us
    pallas_call x1, Pallas kernels, body(): local_call(left_terms_kernel, jax.ShapeDtypeStruct(tie_shape, BF16), [SME...  10.5 us
    unnamed x40, local copies, waits for them, and re-layouts  8.63 us
  transfers between devices with their start and end apart: 4, of which 0 were waited for; matrix products, arithmetic and copies ran while one was open for 4% of the time, Pallas kernels for 44%

profile of v1, /device:TPU:1, one launch (start us, length us, event | category | flops | bytes accessed | tf_op | source)
XLA Modules:
  0.0 230.0 jit_solution(14556369848638765837)
XLA Ops:
  0.6 0.0 copy-start
  0.6 1.6 copy-done
  2.2 0.0 copy-start.16
  2.2 0.0 copy-start.12
  2.2 0.0 copy-start.1
  2.2 0.0 copy-start.8
  2.2 0.0 copy-start.9
  2.3 10.5 %shard_map.175 = bf16[128,64,128]{2,1,0:T(8,128)(2,1)} custom-call(f32[1]{0:T(128)} %bitcast.live, bf16[128,64,128]{2,1,0:T(8,128)(2,1)S(1)} %copy-done, f32[128,64,128]{2,1,0:T(8,128)} %mu.5), custom_call_target="tpu_custom_call" | custom-call | flops 300000000 | bytes 10000000 | tf_op jit(solution)/shard_map/pallas_call | solution.py:204
  12.8 4.5 %collective-permute-start = (bf16[128,64,128]{2,1,0:T(8,128)(2,1)}, bf16[128,64,128]{2,1,0:T(8,128)(2,1)}, u32[]{:S(2)}, u32[]{:S(2)}) collective-permute-start(bf16[128,64,128]{2,1,0:T(8,128)(2,1)} %shard_map.175), channel_id=1, source_target_pairs={{0,1},{1,2},{2,3},{3,4},{4,5},{5,6},{6,7},{8,9},{9,10},{10,11},{11... | collective-permute-start | bytes 6291464 | tf_op jit(solution)/shard_map/ppermute | solution.py:26
  17.9 0.0 copy-done.16
  17.9 0.1 copy.26
  18.1 0.1 reshape.22.pattern
  18.2 0.0 copy-done.12
  18.2 0.1 copy.29
  18.3 0.0 copy-done.1
  18.3 0.0 copy-done.8
  18.3 0.0 copy-done.9
  18.3 0.0 copy-start.2
  18.3 1.9 copy-done.2
  20.2 32.5 %shard_map.174 = (f32[128,64,128]{2,1,0:T(8,128)}, f32[128,64]{1,0:T(8,128)S(1)}) custom-call(f32[1]{0:T(128)} %bitcast.live, s32[1]{0:T(128)S(6)} %copy.34.count, s32[384]{0:T(512)S(1)} %reshape.22.pattern, s32[96]{0:T(128)S(1)} %copy-done.8, s32[128]{0:T(128)S(1)} %copy-done.9, bf16[96,64,320]{2,1,0:T(8,128)(2,1)} %coupling.7, ...), custom_call_target="tpu_custom_call" | custom-call | flops 800000000 | bytes 18000000 | tf_op jit(solution)/shard_map/pallas_call | solution.py:209
  52.6 0.0 copy-start.10
  52.6 0.0 collective-permute-done.received
  52.6 2.6 %broadcast_in_dim.6.cost = f32[128,64,128]{2,1,0:T(8,128)} broadcast(f32[128,64]{1,0:T(8,128)S(1)} %copy.29), dimensions={0,1} | broadcast | bytes 4227072 | tf_op jit(solution)/shard_map/broadcast_in_dim | solution.py:198
  55.2 0.0 copy-done.10
  55.2 0.0 copy-start.13
  55.2 0.0 copy-start.14
  55.2 0.0 copy-start.15
  55.2 10.4 %shard_map.176 = (f32[128,64,128]{2,1,0:T(8,128)}, bf16[128,64,128]{2,1,0:T(8,128)(2,1)S(1)}, bf16[128,64,128]{2,1,0:T(8,128)(2,1)}) custom-call(s32[128]{0:T(128)S(1)} %copy-done.10, bf16[128,64,128]{2,1,0:T(8,128)(2,1)} %collective-permute-done.received, f32[128,64,128]{2,1,0:T(8,128)} %get-tuple-element.21.grad, f32[128,64,128]{2,1,0:T(8,128)} %broadcast_in_dim.6.cost, ...), custom_call_target="tpu_custom_call" | custom-call | flops 10000000 | bytes 25000000 | tf_op jit(solution)/shard_map/pallas_call | solution.py:160
  65.6 0.0 copy-start.6
  65.6 1.3 copy-done.6
  66.9 1.9 collective-permute-start.1
  68.8 0.0 copy-done.13
  68.8 0.1 copy.28
  68.9 0.0 copy-done.14
  68.9 0.1 copy.27
  69.0 0.0 copy-done.15
  69.0 0.1 copy.31
  69.2 15.8 %psum.14 = bf16[128,64]{1,0:T(8,128)(2,1)S(1)} all-reduce(bf16[128,64]{1,0:T(8,128)(2,1)S(1)} %multiply_convert_fusion.1), channel_id=1, replica_groups=mesh['scen'=4,'net'=8] {'scen'}, use_global_device_ids=true, to_apply=%region_0.0 | all-reduce | flops 8192 | bytes 32768 | tf_op jit(solution)/shard_map/psum | solution.py:216
  85.0 0.0 copy-start.7
  85.0 3.4 %convert_add_fusion.target = f32[96,64,128]{2,1,0:T(8,128)} fusion(bf16[96,64,128]{2,1,0:T(8,128)(2,1)} %param.25, f32[96,64]{1,0:T(8,128)S(1)} %copy.31), kind=kLoop, calls=%fused_computation | loop fusion | flops 1572864 | bytes 4743168 | tf_op jit(solution)/shard_map/add | solution.py:199
  88.4 2.2 broadcast_in_dim.7.first
  90.6 0.0 copy-done.7
  90.6 18.7 %shard_map.177 = (f32[96,64,128]{2,1,0:T(8,128)}, f32[128,64,128]{2,1,0:T(8,128)}) custom-call(f32[1]{0:T(128)} %bitcast.live, s32[1]{0:T(128)S(6)} %copy.34.count, s32[384]{0:T(512)S(1)} %reshape.22.pattern, s32[96]{0:T(128)S(1)} %copy-done.8, s32[128]{0:T(128)S(1)} %copy-done.9, bf16[96,64,320]{2,1,0:T(8,128)(2,1)} %coupling.7, ...), custom_call_target="tpu_custom_call" | custom-call | flops 800000000 | bytes 30000000 | tf_op jit(solution)/shard_map/pallas_call | solution.py:222
  109.2 0.0 collective-permute-done.1.arrived
  109.2 0.0 copy-start.3
  109.2 20.7 %shard_map.178 = (f32[128,64,128]{2,1,0:T(8,128)}, bf16[128,64,128]{2,1,0:T(8,128)(2,1)S(1)}) custom-call(f32[1]{0:T(128)} %bitcast.live, bf16[128,64,128]{2,1,0:T(8,128)(2,1)S(1)} %copy-done.1, f32[128,64,128]{2,1,0:T(8,128)} %get-tuple-element.24.mu_part, bf16[128,64,128]{2,1,0:T(8,128)(2,1)} %collective-permute-done.1.arrived), custom_call_target="tpu_custom_call" | custom-call | flops 400000000 | bytes 15000000 | tf_op jit(solution)/shard_map/pallas_call | solution.py:236
  129.9 7.2 %collective-permute-start.2 = (bf16[128,64,128]{2,1,0:T(8,128)(2,1)S(1)}, bf16[128,64,128]{2,1,0:T(8,128)(2,1)S(1)}, u32[]{:S(2)}, u32[]{:S(2)}) collective-permute-start(bf16[128,64,128]{2,1,0:T(8,128)(2,1)S(1)} %get-tuple-element.28), channel_id=1, source_target_pairs={{0,1},{1,2},{2,3},{3,4},{4,5},{5,6},{6,7},{8,9},{9,10},{10,11},{11... | collective-permute-start | bytes 6291464 | tf_op jit(solution)/shard_map/ppermute | solution.py:26
  137.1 0.0 copy-done.3
  137.1 32.5 %shard_map.179 = (f32[128,64,128]{2,1,0:T(8,128)}, f32[128,64]{1,0:T(8,128)S(1)}) custom-call(f32[1]{0:T(128)} %bitcast.live, s32[1]{0:T(128)S(6)} %copy.34.count, s32[384]{0:T(512)S(1)} %reshape.22.pattern, s32[96]{0:T(128)S(1)} %copy-done.8, s32[128]{0:T(128)S(1)} %copy-done.9, bf16[96,64,320]{2,1,0:T(8,128)(2,1)} %coupling.7, ...), custom_call_target="tpu_custom_call" | custom-call | flops 800000000 | bytes 18000000 | tf_op jit(solution)/shard_map/pallas_call | solution.py:209
  169.6 0.0 collective-permute-done.2.received
  169.6 0.0 copy-start.11
  169.6 1.3 copy-done.11
  170.9 10.3 %shard_map.180 = (f32[128,64,128]{2,1,0:T(8,128)}, bf16[128,64,128]{2,1,0:T(8,128)(2,1)S(1)}, bf16[128,64,128]{2,1,0:T(8,128)(2,1)}) custom-call(s32[128]{0:T(128)S(1)} %copy-done.10, bf16[128,64,128]{2,1,0:T(8,128)(2,1)} %copy-done.11, f32[128,64,128]{2,1,0:T(8,128)} %get-tuple-element.29.grad, f32[128,64,128]{2,1,0:T(8,128)} %broadcast_in_dim.6.cost, ...), custom_call_target="tpu_custom_call" | custom-call | flops 10000000 | bytes 25000000 | tf_op jit(solution)/shard_map/pallas_call | solution.py:160
  181.2 0.0 copy-start.4
  181.2 1.3 copy-done.4
  182.5 1.9 collective-permute-start.3
  184.5 12.3 %psum.15 = bf16[128,64]{1,0:T(8,128)(2,1)S(1)} all-reduce(bf16[128,64]{1,0:T(8,128)(2,1)S(1)} %multiply_convert_fusion), channel_id=1, replica_groups=mesh['scen'=4,'net'=8] {'scen'}, use_global_device_ids=true, to_apply=%region_1.2 | all-reduce | flops 8192 | bytes 32768 | tf_op jit(solution)/shard_map/psum | solution.py:216
  196.8 0.7 copy.33
  197.5 0.0 copy-start.5
  197.5 2.2 broadcast_in_dim.8.first
  199.7 0.0 copy-done.5
  199.7 18.6 %shard_map.181 = (f32[96,64,128]{2,1,0:T(8,128)}, f32[128,64,128]{2,1,0:T(8,128)}) custom-call(f32[1]{0:T(128)} %bitcast.live, s32[1]{0:T(128)S(6)} %copy.34.count, s32[384]{0:T(512)S(1)} %reshape.22.pattern, s32[96]{0:T(128)S(1)} %copy-done.8, s32[128]{0:T(128)S(1)} %copy-done.9, bf16[96,64,320]{2,1,0:T(8,128)(2,1)} %coupling.7, ...), custom_call_target="tpu_custom_call" | custom-call | flops 800000000 | bytes 30000000 | tf_op jit(solution)/shard_map/pallas_call | solution.py:222
  218.3 0.0 collective-permute-done.3.arrived
  218.3 11.7 %shard_map.182 = f32[128,64,128]{2,1,0:T(8,128)} custom-call(f32[1]{0:T(128)} %bitcast.live, bf16[128,64,128]{2,1,0:T(8,128)(2,1)S(1)} %copy-done.1, f32[128,64,128]{2,1,0:T(8,128)} %get-tuple-element.34.mu_part, bf16[128,64,128]{2,1,0:T(8,128)(2,1)} %collective-permute-done.3.arrived), custom_call_target="tpu_custom_call" | custom-call | flops 400000000 | bytes 15000000 | tf_op jit(solution)/shard_map/pallas_call | solution.py:236
  (4 shorter events, 0.1 us)
Async XLA Ops:
  0.6 1.6 copy-start
  2.2 15.7 %copy-start.16 = (s32[96,4]{0,1:T(4,128)S(1)}, s32[96,4]{0,1:T(4,128)}, u32[]{:S(2)}) copy-start(s32[96,4]{0,1:T(4,128)} %param.17) | copy-start | bytes 4612
  2.2 15.9 %copy-start.12 = (f32[128,64]{0,1:T(8,128)S(1)}, f32[128,64]{0,1:T(8,128)}, u32[]{:S(2)}) copy-start(f32[128,64]{0,1:T(8,128)} %param.23) | copy-start | bytes 98308
  2.2 16.0 %copy-start.1 = (bf16[128,64,128]{2,1,0:T(8,128)(2,1)S(1)}, bf16[128,64,128]{2,1,0:T(8,128)(2,1)}, u32[]{:S(2)}) copy-start(bf16[128,64,128]{2,1,0:T(8,128)(2,1)} %tie.13) | copy-start | bytes 6291460
  2.2 16.0 %copy-start.8 = (s32[96]{0:T(128)S(1)}, s32[96]{0:T(128)}, u32[]{:S(2)}) copy-start(s32[96]{0:T(128)} %link.7) | copy-start | bytes 1156
  2.2 16.0 %copy-start.9 = (s32[128]{0:T(128)S(1)}, s32[128]{0:T(128)}, u32[]{:S(2)}) copy-start(s32[128]{0:T(128)} %right.7) | copy-start | bytes 1540
  12.8 39.9 %collective-permute-start = (bf16[128,64,128]{2,1,0:T(8,128)(2,1)}, bf16[128,64,128]{2,1,0:T(8,128)(2,1)}, u32[]{:S(2)}, u32[]{:S(2)}) collective-permute-start(bf16[128,64,128]{2,1,0:T(8,128)(2,1)} %shard_map.175), channel_id=1, source_target_pairs={{0,1},{1,2},{2,3},{3,4},{4,5},{5,6},{6,7},{8,9},{9,10},{10,11},{11... | collective-permute-start | bytes 6291464 | tf_op jit(solution)/shard_map/ppermute | solution.py:26
  18.3 1.9 copy-start.2
  52.6 2.6 %copy-start.10 = (s32[128]{0:T(128)S(1)}, s32[128]{0:T(128)}, u32[]{:S(2)}) copy-start(s32[128]{0:T(128)} %left.3) | copy-start | bytes 1540
  55.2 13.6 %copy-start.13 = (f32[128,64]{0,1:T(8,128)S(1)}, f32[128,64]{0,1:T(8,128)}, u32[]{:S(2)}) copy-start(f32[128,64]{0,1:T(8,128)} %param.26) | copy-start | bytes 98308
  55.2 13.7 %copy-start.14 = (f32[128,64]{0,1:T(8,128)S(1)}, f32[128,64]{0,1:T(8,128)}, u32[]{:S(2)}) copy-start(f32[128,64]{0,1:T(8,128)} %param.22) | copy-start | bytes 98308
  55.2 13.8 %copy-start.15 = (f32[96,64]{0,1:T(8,128)S(1)}, f32[96,64]{0,1:T(8,128)}, u32[]{:S(2)}) copy-start(f32[96,64]{0,1:T(8,128)} %param.24) | copy-start | bytes 73732
  65.6 1.3 copy-start.6
  66.9 42.3 %collective-permute-start.1 = (bf16[128,64,128]{2,1,0:T(8,128)(2,1)}, bf16[128,64,128]{2,1,0:T(8,128)(2,1)}, u32[]{:S(2)}, u32[]{:S(2)}) collective-permute-start(bf16[128,64,128]{2,1,0:T(8,128)(2,1)} %get-tuple-element.25), channel_id=1, source_target_pairs={{1,0},{2,1},{3,2},{4,3},{5,4},{6,5},{7,6},{9,8},{10,9},{11,10},{12... | collective-permute-start | bytes 6291464 | tf_op jit(solution)/shard_map/ppermute | solution.py:26
  85.0 5.6 %copy-start.7 = (bf16[128,64,128]{2,1,0:T(8,128)(2,1)S(1)}, bf16[128,64,128]{2,1,0:T(8,128)(2,1)}, u32[]{:S(2)}) copy-start(bf16[128,64,128]{2,1,0:T(8,128)(2,1)} %copy-done.6) | copy-start | bytes 6291460
  109.2 27.9 %copy-start.3 = (f32[96,64,128]{2,1,0:T(8,128)S(1)}, f32[96,64,128]{2,1,0:T(8,128)}, u32[]{:S(2)}) copy-start(f32[96,64,128]{2,1,0:T(8,128)} %get-tuple-element.23.lam) | copy-start | bytes 9437188
  129.9 39.6 %collective-permute-start.2 = (bf16[128,64,128]{2,1,0:T(8,128)(2,1)S(1)}, bf16[128,64,128]{2,1,0:T(8,128)(2,1)S(1)}, u32[]{:S(2)}, u32[]{:S(2)}) collective-permute-start(bf16[128,64,128]{2,1,0:T(8,128)(2,1)S(1)} %get-tuple-element.28), channel_id=1, source_target_pairs={{0,1},{1,2},{2,3},{3,4},{4,5},{5,6},{6,7},{8,9},{9,10},{10,11},{11... | collective-permute-start | bytes 6291464 | tf_op jit(solution)/shard_map/ppermute | solution.py:26
  169.6 1.3 copy-start.11
  181.2 1.3 copy-start.4
  182.5 35.7 %collective-permute-start.3 = (bf16[128,64,128]{2,1,0:T(8,128)(2,1)}, bf16[128,64,128]{2,1,0:T(8,128)(2,1)}, u32[]{:S(2)}, u32[]{:S(2)}) collective-permute-start(bf16[128,64,128]{2,1,0:T(8,128)(2,1)} %get-tuple-element.35), channel_id=1, source_target_pairs={{1,0},{2,1},{3,2},{4,3},{5,4},{6,5},{7,6},{9,8},{10,9},{11,10},{12... | collective-permute-start | bytes 6291464 | tf_op jit(solution)/shard_map/ppermute | solution.py:26
  197.5 2.2 copy-start.5

commit v2 on v1

v2 whole, which is shorter than its diff:
```python
import jax
import jax.numpy as jnp
from jax import lax
from jax.experimental import pallas as pl
from jax.experimental.pallas import tpu as pltpu
from jax.sharding import PartitionSpec as P

BLK = 64
KW = 4
ITERS = 2
UNROLL = 4
STEPS = 8

primal_step = 0.4
first_step = 1.0
dual_step = 0.4

VMEM = pl.BlockSpec(memory_space=pltpu.VMEM)
SMEM = pl.BlockSpec(memory_space=pltpu.SMEM)
F32 = jnp.float32
BF16 = jnp.bfloat16


def from_behind(value, axis, by):
    devices = lax.axis_size(axis)
    pairs = [(i, i + by) for i in range(devices) if 0 <= i + by < devices]
    return lax.ppermute(value, axis, pairs)


def sum_over_scen(value):
    devices = lax.axis_size("scen")
    total = value.astype(F32)
    for by in range(1, devices):
        pairs = [(i, (i + by) % devices) for i in range(devices)]
        total = total + lax.ppermute(value, "scen", pairs).astype(F32)
    return total


def per_step(shape):
    return pl.BlockSpec((shape[0] // STEPS,) + shape[1:], lambda i: (i, 0, 0))


def resident(shape):
    return pl.BlockSpec(shape, lambda i: (0, 0, 0))


def stepped_call(kernel, out_shape, in_specs, out_specs, flops, moved):
    return pl.pallas_call(
        kernel,
        grid=(STEPS,),
        out_shape=out_shape,
        in_specs=in_specs,
        out_specs=out_specs,
        compiler_params=pltpu.CompilerParams(vmem_limit_bytes=48 * 2**20),
        cost_estimate=pl.CostEstimate(flops=flops, bytes_accessed=moved, transcendentals=0),
    )


def rows_loop(count, step, unroll=UNROLL):
    def chunk(c, carry):
        step([c * unroll + u for u in range(unroll)])
        return carry

    lax.fori_loop(0, count // unroll, chunk, 0)


def transposed_dot(a, b):
    return lax.dot_general(a, b, (((0,), (0,)), ((), ())), preferred_element_type=F32)


def zero_first(*refs):
    @pl.when(pl.program_id(0) == 0)
    def _():
        for ref in refs:
            ref[...] = jnp.zeros_like(ref)


def start_terms_kernel(live, right, tie, mu, terms, own):
    base = pl.program_id(0) * tie.shape[0]
    zero_first(own)

    def step(rows):
        parts = [transposed_dot(tie[j], (mu[j] * live[0]).astype(BF16)) for j in rows]
        for j, part in zip(rows, parts):
            terms[j] = part[BLK:].astype(BF16)
            own[right[base + j]] += part[:BLK]

    rows_loop(tie.shape[0], step)


def recourse_kernel(count, pattern, link, coupling, lam, grad, grad_first):
    base = pl.program_id(0) * coupling.shape[0]
    zero_first(grad, grad_first)

    def step(rows):
        halves = [jnp.where(base + r < count[0], lam[r], 0.0).astype(BF16) for r in rows]
        parts = [transposed_dot(coupling[r], h) for r, h in zip(rows, halves)]
        for r, part in zip(rows, parts):
            for k in range(KW):
                grad[pattern[(base + r) * KW + k]] += part[k * BLK : (k + 1) * BLK]
            grad_first[link[base + r]] += part[KW * BLK :]

    rows_loop(coupling.shape[0], step)


def primal_kernel(left, received, grad, own, cost, second, second_next, second_bar, sent, total):
    total[...] = grad[...] + own[...]

    def add_step(rows):
        for j in rows:
            total[left[j]] += received[j].astype(F32)

    rows_loop(received.shape[0], add_step)

    def move_step(rows):
        news = []
        for b in rows:
            now = second[b]
            new = jnp.maximum(now - primal_step * (cost[b] - total[b]), 0.0)
            news.append((new, (2.0 * new - now).astype(BF16)))
        for b, (new, bar) in zip(rows, news):
            second_next[b] = new
            second_bar[b] = bar

    rows_loop(second.shape[0], move_step)

    def gather_step(rows):
        picked = [second_bar[left[j]] for j in rows]
        for j, block in zip(rows, picked):
            sent[j] = block

    rows_loop(received.shape[0], gather_step, 8)


def dual_kernel(count, pattern, link, coupling, bar, first, target, lam, lam_next):
    base = pl.program_id(0) * coupling.shape[0]

    def step(rows):
        news = []
        for r in rows:
            at = base + r
            gathered = [bar[pattern[at * KW + k]] for k in range(KW)] + [first[link[at]]]
            coupled = jnp.dot(coupling[r], jnp.concatenate(gathered, axis=0), preferred_element_type=F32)
            new = lam[r] + dual_step * (target[r] - coupled)
            news.append(jnp.where(at < count[0], new, 0.0))
        for r, new in zip(rows, news):
            lam_next[r] = new

    rows_loop(coupling.shape[0], step)


def tie_kernel(live, right, tie, bar, arrived, mu, mu_next, *more):
    base = pl.program_id(0) * tie.shape[0]
    if more:
        zero_first(more[1])

    def step(rows):
        news = []
        for j in rows:
            stacked = jnp.concatenate([bar[right[base + j]], arrived[j]], axis=0)
            product = jnp.dot(tie[j], stacked, preferred_element_type=F32)
            news.append((mu[j] - dual_step * product) * live[0])
        parts = [transposed_dot(tie[j], new.astype(BF16)) for j, new in zip(rows, news)] if more else []
        for j, new in zip(rows, news):
            mu_next[j] = new
        for j, part in zip(rows, parts):
            more[0][j] = part[BLK:].astype(BF16)
            more[1][right[base + j]] += part[:BLK]

    rows_loop(tie.shape[0], step)


def primal_call(left, received, grad, own, cost, second):
    shape = second.shape
    return pl.pallas_call(
        primal_kernel,
        out_shape=(
            jax.ShapeDtypeStruct(shape, F32),
            jax.ShapeDtypeStruct(shape, BF16),
            jax.ShapeDtypeStruct(received.shape, BF16),
        ),
        in_specs=[SMEM] + [VMEM] * 5,
        out_specs=(VMEM,) * 3,
        scratch_shapes=[pltpu.VMEM(shape, F32)],
        compiler_params=pltpu.CompilerParams(vmem_limit_bytes=48 * 2**20),
        cost_estimate=pl.CostEstimate(flops=10**7, bytes_accessed=25 * 10**6, transcendentals=0),
    )(left, received, grad, own, cost, second)


def body(
    coupling,
    tie_blocks,
    w_pattern,
    link_pattern,
    left_bounds,
    right_bounds,
    block_counts,
    commit_cost,
    dispatch_cost,
    demand,
    wind_error,
    commit_start,
    dispatch_start,
    dual_start,
    tie_start,
):
    scen_dev = dispatch_start.shape[2]
    scen_total = scen_dev * lax.axis_size("scen")
    second_shape = dispatch_start.shape
    tie_shape = tie_start.shape
    wide_shape = commit_start.shape + (scen_dev,)
    live = (lax.axis_index("net") < lax.axis_size("net") - 1).astype(F32).reshape(1)
    pattern = w_pattern.reshape(-1)
    cost = jnp.broadcast_to(dispatch_cost[:, :, None], second_shape)
    target = demand[:, :, None] + wind_error.astype(F32)
    first_now = commit_start
    second_now = dispatch_start
    dual_now = dual_start
    tie_now = tie_start
    second_f32 = jax.ShapeDtypeStruct(second_shape, F32)
    tie_f32 = jax.ShapeDtypeStruct(tie_shape, F32)
    tie_bf16 = jax.ShapeDtypeStruct(tie_shape, BF16)
    dual_f32 = jax.ShapeDtypeStruct(dual_start.shape, F32)
    ties, rows = per_step(tie_shape), per_step(dual_start.shape)
    tie_mats, row_mats = per_step(tie_blocks.shape), per_step(coupling.shape)
    seconds, wides = resident(second_shape), resident(wide_shape)
    terms, own = stepped_call(
        start_terms_kernel,
        (tie_bf16, second_f32),
        [SMEM, SMEM, tie_mats, ties],
        (ties, seconds),
        3 * 10**8,
        13 * 10**6,
    )(live, right_bounds, tie_blocks, tie_start)
    for iteration in range(ITERS):
        received = from_behind(terms, "net", 1)
        grad, grad_wide = stepped_call(
            recourse_kernel,
            (second_f32, jax.ShapeDtypeStruct(wide_shape, F32)),
            [SMEM] * 3 + [row_mats, rows],
            (seconds, wides),
            5 * 10**8,
            16 * 10**6,
        )(block_counts, pattern, link_pattern, coupling, dual_now)
        grad_first = sum_over_scen((jnp.sum(grad_wide, axis=2) / scen_total).astype(BF16))
        second_next, second_bar, sent = primal_call(left_bounds, received, grad, own, cost, second_now)
        sent, grad_first = lax.optimization_barrier((sent, grad_first))
        arrived = from_behind(sent, "net", -1)
        first_next = jnp.clip(first_now - first_step * (commit_cost - grad_first), 0.0, 1.0)
        first_bar = (2.0 * first_next - first_now).astype(BF16)
        first_wide = jnp.broadcast_to(first_bar[:, :, None], wide_shape)
        dual_now = stepped_call(
            dual_kernel,
            dual_f32,
            [SMEM] * 3 + [row_mats, seconds, wides, rows, rows],
            rows,
            5 * 10**8,
            18 * 10**6,
        )(block_counts, pattern, link_pattern, coupling, second_bar, first_wide, target, dual_now)
        arrived, dual_now = lax.optimization_barrier((arrived, dual_now))
        more = iteration < ITERS - 1
        got = stepped_call(
            tie_kernel,
            (tie_f32, tie_bf16, second_f32) if more else (tie_f32,),
            [SMEM, SMEM, tie_mats, seconds, ties, ties],
            (ties, ties, seconds) if more else (ties,),
            6 * 10**8,
            18 * 10**6,
        )(live, right_bounds, tie_blocks, second_bar, arrived, tie_now)
        tie_now = got[0]
        if more:
            terms, own = got[1:]
        first_now = first_next
        second_now = second_next
    return (first_now, second_now, dual_now, tie_now)


def solution(mesh):
    return jax.shard_map(
        body,
        mesh=mesh,
        in_specs=(
            P("net", None, None),
            P("net", None, None),
            P("net", None),
            P("net"),
            P("net"),
            P("net"),
            P("net"),
            P("net", None),
            P("net", None),
            P("net", None),
            P("net", None, "scen"),
            P("net", None),
            P("net", None, "scen"),
            P("net", None, "scen"),
            P("net", None, "scen"),
        ),
        out_specs=(
            P("net", None),
            P("net", None, "scen"),
            P("net", None, "scen"),
            P("net", None, "scen"),
        ),
        check_vma=False,
    )
```

time: 235 us -> 179 us (0.76); the launches traced: 230 us -> 177 us
  Pallas kernels: 166 us -> 106 us
  blocking collectives: 28.1 us -> 0 us
  waiting for transfers between devices: 0.01 us -> 26.3 us
  starting transfers between devices: 15.5 us -> 23.1 us
  other arithmetic: 3.48 us -> 10.1 us
  local copies, waits for them, and re-layouts: 15.7 us -> 10.7 us
    pallas_call x9, Pallas kernels: 166 us -> 106 us  [the longest x2 26.1 us: body(): stepped_call(recourse_kernel, (second_f32, jax.ShapeDtypeStruct(wide_shap...]
    psum x2 -> x0, blocking collectives: 28.1 us -> none  [body(): lax.psum((grad_part / scen_total).astype(BF16), 'scen').astype(F32)]
    ppermute x4, waiting for transfers between devices: 0.01 us -> 22.4 us  [from_behind(): return lax.ppermute(value, axis, pairs)]
    ppermute x0 -> x6, starting transfers between devices: none -> 9.37 us  [sum_over_scen(): total = total + lax.ppermute(value, 'scen', pairs).astype(F32)]
    reduce_sum x0 -> x2, other arithmetic: none -> 6.69 us  [body(): jnp.sum(grad_wide, axis=2) / scen_total]
    ppermute x0 -> x6, waiting for transfers between devices: none -> 3.86 us  [sum_over_scen(): total = total + lax.ppermute(value, 'scen', pairs).astype(F32)]
    unnamed x40 -> x38, local copies, waits for them, and re-layouts: 8.63 us -> 4.77 us
  transfers between devices with their start and end apart: 4 -> 10, of which waited for: 0 -> 7; matrix products, arithmetic and copies ran while one was open for 4% -> 8% of each run, Pallas kernels for 44% -> 26%
where the time goes in v2:
time: 179 us; the launch traced here: 177 us
  Pallas kernels  106 us (59%)
  waiting for transfers between devices  26.3 us (15%)
  starting transfers between devices  23.1 us (13%)
  local copies, waits for them, and re-layouts  10.7 us (6%)
  other arithmetic  10.1 us (6%)
    pallas_call x2, Pallas kernels, body(): stepped_call(recourse_kernel, (second_f32, jax.ShapeDtypeStruct(wide_shap...  26.1 us
    pallas_call x2, Pallas kernels, body(): stepped_call(tie_kernel, (tie_f32, tie_bf16, second_f32) if more else (ti...  24.8 us
    pallas_call x2, Pallas kernels, primal_call(): pl.pallas_call(primal_kernel, out_shape=(jax.ShapeDtypeStruct(shape, F32)...  23.3 us
    ppermute x4, waiting for transfers between devices, from_behind(): return lax.ppermute(value, axis, pairs)  22.4 us
    pallas_call x2, Pallas kernels, body(): stepped_call(dual_kernel, dual_f32, [SMEM] * 3 + [row_mats, seconds, wide...  20.2 us
    ppermute x4, starting transfers between devices, from_behind(): return lax.ppermute(value, axis, pairs)  13.7 us
    pallas_call x1, Pallas kernels, body(): stepped_call(start_terms_kernel, (tie_bf16, second_f32), [SMEM, SMEM, tie...  11.5 us
    ppermute x6, starting transfers between devices, sum_over_scen(): total = total + lax.ppermute(value, 'scen', pairs).astype(F32)  9.37 us
  transfers between devices with their start and end apart: 10, of which 7 were waited for; matrix products, arithmetic and copies ran while one was open for 8% of the time, Pallas kernels for 26%

profile of v2, /device:TPU:1, one launch (start us, length us, event | category | flops | bytes accessed | tf_op | source)
XLA Modules:
  0.0 177.5 jit_solution(7211507059807916725)
XLA Ops:
  0.6 0.0 copy-start.1
  0.7 1.6 copy-done.1
  2.2 0.7 copy-done.7
  2.9 11.5 %shard_map.174 = (bf16[128,64,128]{2,1,0:T(8,128)(2,1)}, f32[128,64,128]{2,1,0:T(8,128)}) custom-call(f32[1]{0:T(128)} %bitcast.live, s32[128]{0:T(128)S(1)} %copy-done.7, bf16[128,64,128]{2,1,0:T(8,128)(2,1)S(1)} %copy-done.1, f32[128,64,128]{2,1,0:T(8,128)} %mu.3), custom_call_target="tpu_custom_call" | custom-call | flops 300000000 | bytes 13000000 | tf_op jit(solution)/shard_map/pallas_call | solution.py:227
  14.4 4.5 %collective-permute-start = (bf16[128,64,128]{2,1,0:T(8,128)(2,1)}, bf16[128,64,128]{2,1,0:T(8,128)(2,1)}, u32[]{:S(2)}, u32[]{:S(2)}) collective-permute-start(bf16[128,64,128]{2,1,0:T(8,128)(2,1)} %get-tuple-element.27), channel_id=1, source_target_pairs={{0,1},{1,2},{2,3},{3,4},{4,5},{5,6},{6,7},{8,9},{9,10},{10,11},{11... | collective-permute-start | bytes 6291464 | tf_op jit(solution)/shard_map/ppermute | solution.py:27
  18.9 0.0 copy-done.15
  18.9 0.1 copy.28
  19.0 0.1 reshape.22.pattern
  19.8 0.0 copy-done.4
  19.8 0.0 copy-done.6
  19.8 13.1 %shard_map.175 = (f32[128,64,128]{2,1,0:T(8,128)}, f32[128,64,128]{2,1,0:T(8,128)}) custom-call(s32[1]{0:T(128)S(6)} %copy.36.count, s32[384]{0:T(512)S(1)} %reshape.22.pattern, s32[96]{0:T(128)S(1)} %copy-done.6, bf16[96,64,320]{2,1,0:T(8,128)(2,1)} %coupling.7, f32[96,64,128]{2,1,0:T(8,128)S(1)} %copy-done.4), custom_call_target="tpu_custom_call" | custom-call | flops 500000000 | bytes 16000000 | tf_op jit(solution)/shard_map/pallas_call | solution.py:237
  32.8 3.3 %reduce_sum.18 = f32[128,64]{1,0:T(8,128)S(1)} reduce(f32[128,64,128]{2,1,0:T(8,128)} %get-tuple-element.31, f32[]{:T(128)} %constant.6.clone.1), dimensions={2}, to_apply=%region_0.0 | reduce | flops 1040384 | bytes 4227076 | tf_op jit(solution)/shard_map/reduce_sum | solution.py:245
  36.2 0.0 copy-start.9
  36.2 1.4 collective-permute-start.1
  37.6 2.3 %collective-permute-start.2 = (bf16[128,64]{1,0:T(8,128)(2,1)S(1)}, bf16[128,64]{1,0:T(8,128)(2,1)S(1)}, u32[]{:S(2)}, u32[]{:S(2)}) collective-permute-start(bf16[128,64]{1,0:T(8,128)(2,1)S(1)} %multiply_convert_fusion.1), channel_id=1, source_target_pairs={{0,16},{8,24},{16,0},{24,8},{1,17},{9,25},{17,1},{25,9},{2,18},{10... | collective-permute-start | bytes 49160 | tf_op jit(solution)/shard_map/ppermute | solution.py:35
  39.9 1.1 collective-permute-start.3
  41.0 0.0 copy-done.11
  41.0 0.1 copy.29
  41.1 0.3 collective-permute-done.1
  41.3 0.3 collective-permute-done.2
  41.6 1.0 collective-permute-done.3
  42.7 0.0 collective-permute-done.received
  42.7 2.6 %broadcast_in_dim.6.cost = f32[128,64,128]{2,1,0:T(8,128)} broadcast(f32[128,64]{1,0:T(8,128)S(1)} %copy.29), dimensions={0,1} | broadcast | bytes 4227072 | tf_op jit(solution)/shard_map/broadcast_in_dim | solution.py:214
  45.3 0.0 copy-done.9
  45.3 11.6 %shard_map.176 = (f32[128,64,128]{2,1,0:T(8,128)}, bf16[128,64,128]{2,1,0:T(8,128)(2,1)S(1)}, bf16[128,64,128]{2,1,0:T(8,128)(2,1)}) custom-call(s32[128]{0:T(128)S(1)} %copy-done.9, bf16[128,64,128]{2,1,0:T(8,128)(2,1)} %collective-permute-done.received, f32[128,64,128]{2,1,0:T(8,128)} %get-tuple-element.28.grad, f32[128,64,128]{2,1,0:T(8,128)} %get-tuple-element.29.own, ...), custom_call_target="tpu_custom_call" | custom-call | flops 10000000 | bytes 25000000 | tf_op jit(solution)/shard_map/pallas_call | solution.py:175
  56.9 3.6 %collective-permute-start.4 = (bf16[128,64,128]{2,1,0:T(8,128)(2,1)}, bf16[128,64,128]{2,1,0:T(8,128)(2,1)}, u32[]{:S(2)}, u32[]{:S(2)}) collective-permute-start(bf16[128,64,128]{2,1,0:T(8,128)(2,1)} %get-tuple-element.34), channel_id=1, source_target_pairs={{1,0},{2,1},{3,2},{4,3},{5,4},{6,5},{7,6},{9,8},{10,9},{11,10},{12... | collective-permute-start | bytes 6291464 | tf_op jit(solution)/shard_map/ppermute | solution.py:27
  60.5 0.0 copy-done.12
  60.5 0.1 copy.30
  60.6 0.0 copy-done.13
  60.7 0.1 copy.31
  60.8 0.0 copy-done.14
  60.8 0.1 copy.33
  60.8 3.3 %convert_add_fusion.target = f32[96,64,128]{2,1,0:T(8,128)} fusion(bf16[96,64,128]{2,1,0:T(8,128)(2,1)} %param.25, f32[96,64]{1,0:T(8,128)S(1)} %copy.33), kind=kLoop, calls=%fused_computation | loop fusion | flops 1572864 | bytes 4743168 | tf_op jit(solution)/shard_map/add | solution.py:215
  64.1 1.6 broadcast_in_dim.7.first
  65.8 0.0 copy-done.5
  65.8 0.0 copy-start.2
  65.8 0.0 copy-start.8
  65.8 10.1 %shard_map.177.lam = f32[96,64,128]{2,1,0:T(8,128)} custom-call(s32[1]{0:T(128)S(6)} %copy.36.count, s32[384]{0:T(512)S(1)} %reshape.22.pattern, s32[96]{0:T(128)S(1)} %copy-done.6, bf16[96,64,320]{2,1,0:T(8,128)(2,1)} %coupling.7, bf16[128,64,128]{2,1,0:T(8,128)(2,1)S(1)} %get-tuple-element.33.bar, bf16[128,64,128]{2,1,0:T(8,128)(2,1)S(1)} %broadcast_in_dim.7.first, ...), custom_call_target="tpu_custom_call" | custom-call | flops 500000000 | bytes 18000000 | tf_op jit(solution)/shard_map/pallas_call | solution.py:252
  75.9 8.9 %collective-permute-done.4.arrived = bf16[128,64,128]{2,1,0:T(8,128)(2,1)} collective-permute-done((bf16[128,64,128]{2,1,0:T(8,128)(2,1)}, bf16[128,64,128]{2,1,0:T(8,128)(2,1)}, u32[]{:S(2)}, u32[]{:S(2)}) %collective-permute-start.4) | collective-permute-done | bytes 2097184 | tf_op jit(solution)/shard_map/ppermute | solution.py:27
  84.8 0.0 copy-done.2
  84.8 0.0 copy-done.8
  84.8 15.2 %shard_map.178 = (f32[128,64,128]{2,1,0:T(8,128)}, bf16[128,64,128]{2,1,0:T(8,128)(2,1)}, f32[128,64,128]{2,1,0:T(8,128)}) custom-call(f32[1]{0:T(128)} %bitcast.live, s32[128]{0:T(128)S(1)} %copy-done.8, bf16[128,64,128]{2,1,0:T(8,128)(2,1)S(1)} %copy-done.2, bf16[128,64,128]{2,1,0:T(8,128)(2,1)} %copy-done.5, ...), custom_call_target="tpu_custom_call" | custom-call | flops 600000000 | bytes 18000000 | tf_op jit(solution)/shard_map/pallas_call | solution.py:262
  100.0 1.9 %collective-permute-start.5 = (bf16[128,64,128]{2,1,0:T(8,128)(2,1)}, bf16[128,64,128]{2,1,0:T(8,128)(2,1)S(1)}, u32[]{:S(2)}, u32[]{:S(2)}) collective-permute-start(bf16[128,64,128]{2,1,0:T(8,128)(2,1)} %get-tuple-element.36), channel_id=1, source_target_pairs={{0,1},{1,2},{2,3},{3,4},{4,5},{5,6},{6,7},{8,9},{9,10},{10,11},{11... | collective-permute-start | bytes 6291464 | tf_op jit(solution)/shard_map/ppermute | solution.py:27
  101.9 0.0 copy-done
  101.9 13.1 %shard_map.179 = (f32[128,64,128]{2,1,0:T(8,128)}, f32[128,64,128]{2,1,0:T(8,128)}) custom-call(s32[1]{0:T(128)S(6)} %copy.36.count, s32[384]{0:T(512)S(1)} %reshape.22.pattern, s32[96]{0:T(128)S(1)} %copy-done.6, bf16[96,64,320]{2,1,0:T(8,128)(2,1)} %coupling.7, f32[96,64,128]{2,1,0:T(8,128)S(1)} %copy-done), custom_call_target="tpu_custom_call" | custom-call | flops 500000000 | bytes 16000000 | tf_op jit(solution)/shard_map/pallas_call | solution.py:237
  115.0 3.3 %reduce_sum.19 = f32[128,64]{1,0:T(8,128)S(1)} reduce(f32[128,64,128]{2,1,0:T(8,128)} %get-tuple-element.42, f32[]{:T(128)} %constant.6.clone.1), dimensions={2}, to_apply=%region_1.2 | reduce | flops 1040384 | bytes 4227076 | tf_op jit(solution)/shard_map/reduce_sum | solution.py:245
  118.4 1.3 collective-permute-start.6
  119.6 2.3 %collective-permute-start.7 = (bf16[128,64]{1,0:T(8,128)(2,1)S(1)}, bf16[128,64]{1,0:T(8,128)(2,1)S(1)}, u32[]{:S(2)}, u32[]{:S(2)}) collective-permute-start(bf16[128,64]{1,0:T(8,128)(2,1)S(1)} %multiply_convert_fusion), channel_id=1, source_target_pairs={{0,16},{8,24},{16,0},{24,8},{1,17},{9,25},{17,1},{25,9},{2,18},{10... | collective-permute-start | bytes 49160 | tf_op jit(solution)/shard_map/ppermute | solution.py:35
  121.9 1.1 collective-permute-start.8
  123.0 0.0 collective-permute-done.6
  123.0 0.3 collective-permute-done.7
  123.3 1.9 %collective-permute-done.8 = bf16[128,64]{1,0:T(8,128)(2,1)S(1)} collective-permute-done((bf16[128,64]{1,0:T(8,128)(2,1)S(1)}, bf16[128,64]{1,0:T(8,128)(2,1)S(1)}, u32[]{:S(2)}, u32[]{:S(2)}) %collective-permute-start.8) | collective-permute-done | bytes 16416 | tf_op jit(solution)/shard_map/ppermute | solution.py:35
  125.3 0.0 collective-permute-done.5.received
  125.3 0.0 copy-start.10
  125.3 1.3 copy-done.10
  126.6 11.7 %shard_map.180 = (f32[128,64,128]{2,1,0:T(8,128)}, bf16[128,64,128]{2,1,0:T(8,128)(2,1)S(1)}, bf16[128,64,128]{2,1,0:T(8,128)(2,1)}) custom-call(s32[128]{0:T(128)S(1)} %copy-done.9, bf16[128,64,128]{2,1,0:T(8,128)(2,1)} %copy-done.10, f32[128,64,128]{2,1,0:T(8,128)} %get-tuple-element.38.grad, f32[128,64,128]{2,1,0:T(8,128)} %get-tuple-element.39.own, ...), custom_call_target="tpu_custom_call" | custom-call | flops 10000000 | bytes 25000000 | tf_op jit(solution)/shard_map/pallas_call | solution.py:175
  138.3 3.7 %collective-permute-start.9 = (bf16[128,64,128]{2,1,0:T(8,128)(2,1)}, bf16[128,64,128]{2,1,0:T(8,128)(2,1)}, u32[]{:S(2)}, u32[]{:S(2)}) collective-permute-start(bf16[128,64,128]{2,1,0:T(8,128)(2,1)} %get-tuple-element.45), channel_id=1, source_target_pairs={{1,0},{2,1},{3,2},{4,3},{5,4},{6,5},{7,6},{9,8},{10,9},{11,10},{12... | collective-permute-start | bytes 6291464 | tf_op jit(solution)/shard_map/ppermute | solution.py:27
  142.0 0.7 copy.35
  142.7 1.6 broadcast_in_dim.8.first
  144.3 0.0 copy-start.3
  144.3 10.1 %shard_map.181 = f32[96,64,128]{2,1,0:T(8,128)} custom-call(s32[1]{0:T(128)S(6)} %copy.36.count, s32[384]{0:T(512)S(1)} %reshape.22.pattern, s32[96]{0:T(128)S(1)} %copy-done.6, bf16[96,64,320]{2,1,0:T(8,128)(2,1)} %coupling.7, bf16[128,64,128]{2,1,0:T(8,128)(2,1)S(1)} %get-tuple-element.46.bar, bf16[128,64,128]{2,1,0:T(8,128)(2,1)S(1)} %broadcast_in_dim.8.first, ...), custom_call_target="tpu_custom_call" | custom-call | flops 500000000 | bytes 18000000 | tf_op jit(solution)/shard_map/pallas_call | solution.py:252
  154.4 13.4 %collective-permute-done.9.arrived = bf16[128,64,128]{2,1,0:T(8,128)(2,1)} collective-permute-done((bf16[128,64,128]{2,1,0:T(8,128)(2,1)}, bf16[128,64,128]{2,1,0:T(8,128)(2,1)}, u32[]{:S(2)}, u32[]{:S(2)}) %collective-permute-start.9) | collective-permute-done | bytes 2097184 | tf_op jit(solution)/shard_map/ppermute | solution.py:27
  167.8 0.0 copy-done.3
  167.8 9.7 %shard_map.182 = f32[128,64,128]{2,1,0:T(8,128)} custom-call(f32[1]{0:T(128)} %bitcast.live, s32[128]{0:T(128)S(1)} %copy-done.8, bf16[128,64,128]{2,1,0:T(8,128)(2,1)S(1)} %copy-done.3, bf16[128,64,128]{2,1,0:T(8,128)(2,1)S(1)} %get-tuple-element.46.bar, bf16[128,64,128]{2,1,0:T(8,128)(2,1)} %collective-permute-done.9.arrived, ...), custom_call_target="tpu_custom_call" | custom-call | flops 600000000 | bytes 18000000 | tf_op jit(solution)/shard_map/pallas_call | solution.py:262
  (16 shorter events, 0.1 us)
Async XLA Ops:
  0.6 1.6 copy-start.1
  2.2 0.7 copy-start.7
  2.9 16.0 %copy-start.15 = (s32[96,4]{0,1:T(4,128)S(1)}, s32[96,4]{0,1:T(4,128)}, u32[]{:S(2)}) copy-start(s32[96,4]{0,1:T(4,128)} %param.17) | copy-start | bytes 4612
  2.9 16.9 %copy-start.4 = (f32[96,64,128]{2,1,0:T(8,128)S(1)}, f32[96,64,128]{2,1,0:T(8,128)}, u32[]{:S(2)}) copy-start(f32[96,64,128]{2,1,0:T(8,128)} %lam.3) | copy-start | bytes 9437188
  2.9 16.9 %copy-start.6 = (s32[96]{0:T(128)S(1)}, s32[96]{0:T(128)}, u32[]{:S(2)}) copy-start(s32[96]{0:T(128)} %link.7) | copy-start | bytes 1156
  14.4 28.3 %collective-permute-start = (bf16[128,64,128]{2,1,0:T(8,128)(2,1)}, bf16[128,64,128]{2,1,0:T(8,128)(2,1)}, u32[]{:S(2)}, u32[]{:S(2)}) collective-permute-start(bf16[128,64,128]{2,1,0:T(8,128)(2,1)} %get-tuple-element.27), channel_id=1, source_target_pairs={{0,1},{1,2},{2,3},{3,4},{4,5},{5,6},{6,7},{8,9},{9,10},{10,11},{11... | collective-permute-start | bytes 6291464 | tf_op jit(solution)/shard_map/ppermute | solution.py:27
  32.8 8.1 %copy-start.11 = (f32[128,64]{0,1:T(8,128)S(1)}, f32[128,64]{0,1:T(8,128)}, u32[]{:S(2)}) copy-start(f32[128,64]{0,1:T(8,128)} %param.23) | copy-start | bytes 98308
  36.2 9.1 %copy-start.9 = (s32[128]{0:T(128)S(1)}, s32[128]{0:T(128)}, u32[]{:S(2)}) copy-start(s32[128]{0:T(128)} %left.3) | copy-start | bytes 1540
  36.2 5.1 %collective-permute-start.1 = (bf16[128,64]{1,0:T(8,128)(2,1)S(1)}, bf16[128,64]{1,0:T(8,128)(2,1)S(1)}, u32[]{:S(2)}, u32[]{:S(2)}) collective-permute-start(bf16[128,64]{1,0:T(8,128)(2,1)S(1)} %multiply_convert_fusion.1), channel_id=1, source_target_pairs={{0,8},{8,16},{16,24},{24,0},{1,9},{9,17},{17,25},{25,1},{2,10},{10... | collective-permute-start | bytes 49160 | tf_op jit(solution)/shard_map/ppermute | solution.py:35
  37.6 4.0 %collective-permute-start.2 = (bf16[128,64]{1,0:T(8,128)(2,1)S(1)}, bf16[128,64]{1,0:T(8,128)(2,1)S(1)}, u32[]{:S(2)}, u32[]{:S(2)}) collective-permute-start(bf16[128,64]{1,0:T(8,128)(2,1)S(1)} %multiply_convert_fusion.1), channel_id=1, source_target_pairs={{0,16},{8,24},{16,0},{24,8},{1,17},{9,25},{17,1},{25,9},{2,18},{10... | collective-permute-start | bytes 49160 | tf_op jit(solution)/shard_map/ppermute | solution.py:35
  39.9 2.8 %collective-permute-start.3 = (bf16[128,64]{1,0:T(8,128)(2,1)S(1)}, bf16[128,64]{1,0:T(8,128)(2,1)S(1)}, u32[]{:S(2)}, u32[]{:S(2)}) collective-permute-start(bf16[128,64]{1,0:T(8,128)(2,1)S(1)} %multiply_convert_fusion.1), channel_id=1, source_target_pairs={{0,24},{8,0},{16,8},{24,16},{1,25},{9,1},{17,9},{25,17},{2,26},{10... | collective-permute-start | bytes 49160 | tf_op jit(solution)/shard_map/ppermute | solution.py:35
  45.3 15.3 %copy-start.12 = (f32[128,64]{0,1:T(8,128)S(1)}, f32[128,64]{0,1:T(8,128)}, u32[]{:S(2)}) copy-start(f32[128,64]{0,1:T(8,128)} %param.22) | copy-start | bytes 98308
  45.3 15.4 %copy-start.13 = (f32[128,64]{0,1:T(8,128)S(1)}, f32[128,64]{0,1:T(8,128)}, u32[]{:S(2)}) copy-start(f32[128,64]{0,1:T(8,128)} %param.26) | copy-start | bytes 98308
  45.3 15.5 %copy-start.14 = (f32[96,64]{0,1:T(8,128)S(1)}, f32[96,64]{0,1:T(8,128)}, u32[]{:S(2)}) copy-start(f32[96,64]{0,1:T(8,128)} %param.24) | copy-start | bytes 73732
  56.9 8.9 %copy-start.5 = (bf16[128,64,128]{2,1,0:T(8,128)(2,1)}, bf16[128,64,128]{2,1,0:T(8,128)(2,1)S(1)}, u32[]{:S(2)}) copy-start(bf16[128,64,128]{2,1,0:T(8,128)(2,1)S(1)} %get-tuple-element.33.bar) | copy-start | bytes 6291460
  56.9 27.9 %collective-permute-start.4 = (bf16[128,64,128]{2,1,0:T(8,128)(2,1)}, bf16[128,64,128]{2,1,0:T(8,128)(2,1)}, u32[]{:S(2)}, u32[]{:S(2)}) collective-permute-start(bf16[128,64,128]{2,1,0:T(8,128)(2,1)} %get-tuple-element.34), channel_id=1, source_target_pairs={{1,0},{2,1},{3,2},{4,3},{5,4},{6,5},{7,6},{9,8},{10,9},{11,10},{12... | collective-permute-start | bytes 6291464 | tf_op jit(solution)/shard_map/ppermute | solution.py:27
  65.8 19.1 %copy-start.2 = (bf16[128,64,128]{2,1,0:T(8,128)(2,1)S(1)}, bf16[128,64,128]{2,1,0:T(8,128)(2,1)}, u32[]{:S(2)}) copy-start(bf16[128,64,128]{2,1,0:T(8,128)(2,1)} %tie.5) | copy-start | bytes 6291460
  65.8 19.0 %copy-start.8 = (s32[128]{0:T(128)S(1)}, s32[128]{0:T(128)}, u32[]{:S(2)}) copy-start(s32[128]{0:T(128)} %right.5) | copy-start | bytes 1540
  75.9 26.0 %copy-start = (f32[96,64,128]{2,1,0:T(8,128)S(1)}, f32[96,64,128]{2,1,0:T(8,128)}, u32[]{:S(2)}) copy-start(f32[96,64,128]{2,1,0:T(8,128)} %shard_map.177.lam) | copy-start | bytes 9437188
  100.0 25.3 %collective-permute-start.5 = (bf16[128,64,128]{2,1,0:T(8,128)(2,1)}, bf16[128,64,128]{2,1,0:T(8,128)(2,1)S(1)}, u32[]{:S(2)}, u32[]{:S(2)}) collective-permute-start(bf16[128,64,128]{2,1,0:T(8,128)(2,1)} %get-tuple-element.36), channel_id=1, source_target_pairs={{0,1},{1,2},{2,3},{3,4},{4,5},{5,6},{6,7},{8,9},{9,10},{10,11},{11... | collective-permute-start | bytes 6291464 | tf_op jit(solution)/shard_map/ppermute | solution.py:27
  118.4 4.6 %collective-permute-start.6 = (bf16[128,64]{1,0:T(8,128)(2,1)S(1)}, bf16[128,64]{1,0:T(8,128)(2,1)S(1)}, u32[]{:S(2)}, u32[]{:S(2)}) collective-permute-start(bf16[128,64]{1,0:T(8,128)(2,1)S(1)} %multiply_convert_fusion), channel_id=1, source_target_pairs={{0,8},{8,16},{16,24},{24,0},{1,9},{9,17},{17,25},{25,1},{2,10},{10... | collective-permute-start | bytes 49160 | tf_op jit(solution)/shard_map/ppermute | solution.py:35
  119.6 3.7 %collective-permute-start.7 = (bf16[128,64]{1,0:T(8,128)(2,1)S(1)}, bf16[128,64]{1,0:T(8,128)(2,1)S(1)}, u32[]{:S(2)}, u32[]{:S(2)}) collective-permute-start(bf16[128,64]{1,0:T(8,128)(2,1)S(1)} %multiply_convert_fusion), channel_id=1, source_target_pairs={{0,16},{8,24},{16,0},{24,8},{1,17},{9,25},{17,1},{25,9},{2,18},{10... | collective-permute-start | bytes 49160 | tf_op jit(solution)/shard_map/ppermute | solution.py:35
  121.9 3.3 %collective-permute-start.8 = (bf16[128,64]{1,0:T(8,128)(2,1)S(1)}, bf16[128,64]{1,0:T(8,128)(2,1)S(1)}, u32[]{:S(2)}, u32[]{:S(2)}) collective-permute-start(bf16[128,64]{1,0:T(8,128)(2,1)S(1)} %multiply_convert_fusion), channel_id=1, source_target_pairs={{0,24},{8,0},{16,8},{24,16},{1,25},{9,1},{17,9},{25,17},{2,26},{10... | collective-permute-start | bytes 49160 | tf_op jit(solution)/shard_map/ppermute | solution.py:35
  125.3 1.3 copy-start.10
  138.3 29.6 %collective-permute-start.9 = (bf16[128,64,128]{2,1,0:T(8,128)(2,1)}, bf16[128,64,128]{2,1,0:T(8,128)(2,1)}, u32[]{:S(2)}, u32[]{:S(2)}) collective-permute-start(bf16[128,64,128]{2,1,0:T(8,128)(2,1)} %get-tuple-element.45), channel_id=1, source_target_pairs={{1,0},{2,1},{3,2},{4,3},{5,4},{6,5},{7,6},{9,8},{10,9},{11,10},{12... | collective-permute-start | bytes 6291464 | tf_op jit(solution)/shard_map/ppermute | solution.py:27
  144.3 23.5 %copy-start.3 = (bf16[128,64,128]{2,1,0:T(8,128)(2,1)S(1)}, bf16[128,64,128]{2,1,0:T(8,128)(2,1)}, u32[]{:S(2)}) copy-start(bf16[128,64,128]{2,1,0:T(8,128)(2,1)} %tie.5) | copy-start | bytes 6291460

commit v3 on v2

--- a/solution.py
+++ b/solution.py
@@ -8,8 +8,8 @@
 BLK = 64
 KW = 4
 ITERS = 2
-UNROLL = 4
-STEPS = 8
+UNROLL = 32
+STEPS = 4
 
 primal_step = 0.4
 first_step = 1.0
@@ -57,6 +57,8 @@
 
 
 def rows_loop(count, step, unroll=UNROLL):
+    unroll = max(u for u in range(1, unroll + 1) if count % u == 0)
+
     def chunk(c, carry):
         step([c * unroll + u for u in range(unroll)])
         return carry
@@ -83,6 +85,7 @@
         parts = [transposed_dot(tie[j], (mu[j] * live[0]).astype(BF16)) for j in rows]
         for j, part in zip(rows, parts):
             terms[j] = part[BLK:].astype(BF16)
+        for j, part in zip(rows, parts):
             own[right[base + j]] += part[:BLK]
 
     rows_loop(tie.shape[0], step)
@@ -110,7 +113,7 @@
         for j in rows:
             total[left[j]] += received[j].astype(F32)
 
-    rows_loop(received.shape[0], add_step)
+    rows_loop(received.shape[0], add_step, 8)
 
     def move_step(rows):
         news = []
@@ -122,14 +125,14 @@
             second_next[b] = new
             second_bar[b] = bar
 
-    rows_loop(second.shape[0], move_step)
+    rows_loop(second.shape[0], move_step, 8)
 
     def gather_step(rows):
         picked = [second_bar[left[j]] for j in rows]
         for j, block in zip(rows, picked):
             sent[j] = block
 
-    rows_loop(received.shape[0], gather_step, 8)
+    rows_loop(received.shape[0], gather_step, 16)
 
 
 def dual_kernel(count, pattern, link, coupling, bar, first, target, lam, lam_next):

time: 179 us -> 163 us (0.911)
  Pallas kernels: 106 us -> 78 us
  waiting for transfers between devices: 26.3 us -> 41.7 us
  starting transfers between devices: 23.1 us -> 19.7 us
    ppermute x4, waiting for transfers between devices: 22.4 us -> 37.8 us  [from_behind(): return lax.ppermute(value, axis, pairs)]
    pallas_call x2, Pallas kernels: 24.8 us -> 15.4 us  [body(): stepped_call(tie_kernel, (tie_f32, tie_bf16, second_f32) if more else (ti...]
    pallas_call x2, Pallas kernels: 26.1 us -> 18.6 us  [body(): stepped_call(recourse_kernel, (second_f32, jax.ShapeDtypeStruct(wide_shap...]
    pallas_call x2, Pallas kernels: 20.2 us -> 14.3 us  [body(): stepped_call(dual_kernel, dual_f32, [SMEM] * 3 + [row_mats, seconds, wide...]
    pallas_call x1, Pallas kernels: 11.5 us -> 6.93 us  [body(): stepped_call(start_terms_kernel, (tie_bf16, second_f32), [SMEM, SMEM, tie...]
    ppermute x4, starting transfers between devices: 13.7 us -> 10.2 us  [from_behind(): return lax.ppermute(value, axis, pairs)]
  transfers between devices with their start and end apart: 10 -> 10, of which waited for: 7 -> 9; matrix products, arithmetic and copies ran while one was open for 8% -> 9% of each run, Pallas kernels for 26% -> 20%
where the time goes in v3:
time: 163 us; the launch traced here: 162 us
  Pallas kernels  78 us (48%)
  waiting for transfers between devices  41.7 us (26%)
  starting transfers between devices  19.7 us (12%)
  local copies, waits for them, and re-layouts  10.7 us (7%)
  other arithmetic  10.1 us (6%)
    ppermute x4, waiting for transfers between devices, from_behind(): return lax.ppermute(value, axis, pairs)  37.8 us
    pallas_call x2, Pallas kernels, primal_call(): pl.pallas_call(primal_kernel, out_shape=(jax.ShapeDtypeStruct(shape, F32)...  22.8 us
    pallas_call x2, Pallas kernels, body(): stepped_call(recourse_kernel, (second_f32, jax.ShapeDtypeStruct(wide_shap...  18.6 us
    pallas_call x2, Pallas kernels, body(): stepped_call(tie_kernel, (tie_f32, tie_bf16, second_f32) if more else (ti...  15.4 us
    pallas_call x2, Pallas kernels, body(): stepped_call(dual_kernel, dual_f32, [SMEM] * 3 + [row_mats, seconds, wide...  14.3 us
    ppermute x4, starting transfers between devices, from_behind(): return lax.ppermute(value, axis, pairs)  10.2 us
    ppermute x6, starting transfers between devices, sum_over_scen(): total = total + lax.ppermute(value, 'scen', pairs).astype(F32)  9.44 us
    pallas_call x1, Pallas kernels, body(): stepped_call(start_terms_kernel, (tie_bf16, second_f32), [SMEM, SMEM, tie...  6.93 us
  transfers between devices with their start and end apart: 10, of which 9 were waited for; matrix products, arithmetic and copies ran while one was open for 9% of the time, Pallas kernels for 20%

profile of v3, /device:TPU:1, one launch (start us, length us, event | category | flops | bytes accessed | tf_op | source)
XLA Modules:
  0.0 161.7 jit_solution(1625653569355367305)
XLA Ops:
  0.6 0.0 copy-start.1
  0.7 1.6 copy-done.1
  2.2 0.0 copy-start.7
  2.2 0.7 copy-done.7
  2.9 6.9 %shard_map.174 = (bf16[128,64,128]{2,1,0:T(8,128)(2,1)}, f32[128,64,128]{2,1,0:T(8,128)}) custom-call(f32[1]{0:T(128)} %bitcast.live, s32[128]{0:T(128)S(1)} %copy-done.7, bf16[128,64,128]{2,1,0:T(8,128)(2,1)S(1)} %copy-done.1, f32[128,64,128]{2,1,0:T(8,128)} %mu.3), custom_call_target="tpu_custom_call" | custom-call | flops 300000000 | bytes 13000000 | tf_op jit(solution)/shard_map/pallas_call | solution.py:230
  9.8 4.5 %collective-permute-start = (bf16[128,64,128]{2,1,0:T(8,128)(2,1)}, bf16[128,64,128]{2,1,0:T(8,128)(2,1)}, u32[]{:S(2)}, u32[]{:S(2)}) collective-permute-start(bf16[128,64,128]{2,1,0:T(8,128)(2,1)} %get-tuple-element.27), channel_id=1, source_target_pairs={{0,1},{1,2},{2,3},{3,4},{4,5},{5,6},{6,7},{8,9},{9,10},{10,11},{11... | collective-permute-start | bytes 6291464 | tf_op jit(solution)/shard_map/ppermute | solution.py:27
  14.3 0.0 copy-done.15
  14.3 0.1 copy.28
  14.5 0.1 reshape.22.pattern
  15.2 0.0 copy-done.4
  15.2 0.0 copy-done.6
  15.2 9.3 %shard_map.175 = (f32[128,64,128]{2,1,0:T(8,128)}, f32[128,64,128]{2,1,0:T(8,128)}) custom-call(s32[1]{0:T(128)S(6)} %copy.36.count, s32[384]{0:T(512)S(1)} %reshape.22.pattern, s32[96]{0:T(128)S(1)} %copy-done.6, bf16[96,64,320]{2,1,0:T(8,128)(2,1)} %coupling.7, f32[96,64,128]{2,1,0:T(8,128)S(1)} %copy-done.4), custom_call_target="tpu_custom_call" | custom-call | flops 500000000 | bytes 16000000 | tf_op jit(solution)/shard_map/pallas_call | solution.py:240
  24.5 3.3 %reduce_sum.18 = f32[128,64]{1,0:T(8,128)S(1)} reduce(f32[128,64,128]{2,1,0:T(8,128)} %get-tuple-element.31, f32[]{:T(128)} %constant.6.clone.1), dimensions={2}, to_apply=%region_0.0 | reduce | flops 1040384 | bytes 4227076 | tf_op jit(solution)/shard_map/reduce_sum | solution.py:248
  27.9 0.0 copy-start.9
  27.9 1.3 collective-permute-start.1
  29.2 2.3 %collective-permute-start.2 = (bf16[128,64]{1,0:T(8,128)(2,1)S(1)}, bf16[128,64]{1,0:T(8,128)(2,1)S(1)}, u32[]{:S(2)}, u32[]{:S(2)}) collective-permute-start(bf16[128,64]{1,0:T(8,128)(2,1)S(1)} %multiply_convert_fusion.1), channel_id=1, source_target_pairs={{0,16},{8,24},{16,0},{24,8},{1,17},{9,25},{17,1},{25,9},{2,18},{10... | collective-permute-start | bytes 49160 | tf_op jit(solution)/shard_map/ppermute | solution.py:35
  31.6 1.1 collective-permute-start.3
  32.6 0.0 copy-done.11
  32.6 0.1 copy.29
  32.7 0.3 collective-permute-done.1
  33.0 0.3 collective-permute-done.2
  33.3 1.0 collective-permute-done.3
  34.3 3.3 %collective-permute-done.received = bf16[128,64,128]{2,1,0:T(8,128)(2,1)} collective-permute-done((bf16[128,64,128]{2,1,0:T(8,128)(2,1)}, bf16[128,64,128]{2,1,0:T(8,128)(2,1)}, u32[]{:S(2)}, u32[]{:S(2)}) %collective-permute-start) | collective-permute-done | bytes 2097184 | tf_op jit(solution)/shard_map/ppermute | solution.py:27
  37.6 2.6 %broadcast_in_dim.6.cost = f32[128,64,128]{2,1,0:T(8,128)} broadcast(f32[128,64]{1,0:T(8,128)S(1)} %copy.29), dimensions={0,1} | broadcast | bytes 4227072 | tf_op jit(solution)/shard_map/broadcast_in_dim | solution.py:217
  40.2 0.0 copy-done.9
  40.2 11.4 %shard_map.176 = (f32[128,64,128]{2,1,0:T(8,128)}, bf16[128,64,128]{2,1,0:T(8,128)(2,1)S(1)}, bf16[128,64,128]{2,1,0:T(8,128)(2,1)}) custom-call(s32[128]{0:T(128)S(1)} %copy-done.9, bf16[128,64,128]{2,1,0:T(8,128)(2,1)} %collective-permute-done.received, f32[128,64,128]{2,1,0:T(8,128)} %get-tuple-element.28.grad, f32[128,64,128]{2,1,0:T(8,128)} %get-tuple-element.29.own, ...), custom_call_target="tpu_custom_call" | custom-call | flops 10000000 | bytes 25000000 | tf_op jit(solution)/shard_map/pallas_call | solution.py:178
  51.6 1.9 %collective-permute-start.4 = (bf16[128,64,128]{2,1,0:T(8,128)(2,1)}, bf16[128,64,128]{2,1,0:T(8,128)(2,1)}, u32[]{:S(2)}, u32[]{:S(2)}) collective-permute-start(bf16[128,64,128]{2,1,0:T(8,128)(2,1)} %get-tuple-element.34), channel_id=1, source_target_pairs={{1,0},{2,1},{3,2},{4,3},{5,4},{6,5},{7,6},{9,8},{10,9},{11,10},{12... | collective-permute-start | bytes 6291464 | tf_op jit(solution)/shard_map/ppermute | solution.py:27
  53.5 0.0 copy-done.12
  53.5 0.1 copy.30
  53.6 0.0 copy-done.13
  53.6 0.1 copy.31
  53.7 0.0 copy-done.14
  53.7 0.1 copy.33
  53.8 3.3 %convert_add_fusion.target = f32[96,64,128]{2,1,0:T(8,128)} fusion(bf16[96,64,128]{2,1,0:T(8,128)(2,1)} %param.25, f32[96,64]{1,0:T(8,128)S(1)} %copy.33), kind=kLoop, calls=%fused_computation | loop fusion | flops 1572864 | bytes 4743168 | tf_op jit(solution)/shard_map/add | solution.py:218
  57.1 1.6 %broadcast_in_dim.7.first = bf16[128,64,128]{2,1,0:T(8,128)(2,1)S(1)} broadcast(bf16[128,64]{1,0:T(8,128)(2,1)S(1)} %subtract_convert_fusion.1), dimensions={0,1} | broadcast | bytes 2113536 | tf_op jit(solution)/shard_map/broadcast_in_dim | solution.py:254
  58.7 0.0 copy-done.5
  58.7 0.0 copy-start.2
  58.7 0.0 copy-start.8
  58.8 7.1 %shard_map.177.lam = f32[96,64,128]{2,1,0:T(8,128)} custom-call(s32[1]{0:T(128)S(6)} %copy.36.count, s32[384]{0:T(512)S(1)} %reshape.22.pattern, s32[96]{0:T(128)S(1)} %copy-done.6, bf16[96,64,320]{2,1,0:T(8,128)(2,1)} %coupling.7, bf16[128,64,128]{2,1,0:T(8,128)(2,1)S(1)} %get-tuple-element.33.bar, bf16[128,64,128]{2,1,0:T(8,128)(2,1)S(1)} %broadcast_in_dim.7.first, ...), custom_call_target="tpu_custom_call" | custom-call | flops 500000000 | bytes 18000000 | tf_op jit(solution)/shard_map/pallas_call | solution.py:255
  65.9 14.1 %collective-permute-done.4.arrived = bf16[128,64,128]{2,1,0:T(8,128)(2,1)} collective-permute-done((bf16[128,64,128]{2,1,0:T(8,128)(2,1)}, bf16[128,64,128]{2,1,0:T(8,128)(2,1)}, u32[]{:S(2)}, u32[]{:S(2)}) %collective-permute-start.4) | collective-permute-done | bytes 2097184 | tf_op jit(solution)/shard_map/ppermute | solution.py:27
  80.0 0.0 copy-done.2
  80.0 0.0 copy-done.8
  80.0 9.5 %shard_map.178 = (f32[128,64,128]{2,1,0:T(8,128)}, bf16[128,64,128]{2,1,0:T(8,128)(2,1)}, f32[128,64,128]{2,1,0:T(8,128)}) custom-call(f32[1]{0:T(128)} %bitcast.live, s32[128]{0:T(128)S(1)} %copy-done.8, bf16[128,64,128]{2,1,0:T(8,128)(2,1)S(1)} %copy-done.2, bf16[128,64,128]{2,1,0:T(8,128)(2,1)} %copy-done.5, ...), custom_call_target="tpu_custom_call" | custom-call | flops 600000000 | bytes 18000000 | tf_op jit(solution)/shard_map/pallas_call | solution.py:265
  89.5 1.9 %collective-permute-start.5 = (bf16[128,64,128]{2,1,0:T(8,128)(2,1)}, bf16[128,64,128]{2,1,0:T(8,128)(2,1)S(1)}, u32[]{:S(2)}, u32[]{:S(2)}) collective-permute-start(bf16[128,64,128]{2,1,0:T(8,128)(2,1)} %get-tuple-element.36), channel_id=1, source_target_pairs={{0,1},{1,2},{2,3},{3,4},{4,5},{5,6},{6,7},{8,9},{9,10},{10,11},{11... | collective-permute-start | bytes 6291464 | tf_op jit(solution)/shard_map/ppermute | solution.py:27
  91.4 0.0 copy-done
  91.4 9.3 %shard_map.179 = (f32[128,64,128]{2,1,0:T(8,128)}, f32[128,64,128]{2,1,0:T(8,128)}) custom-call(s32[1]{0:T(128)S(6)} %copy.36.count, s32[384]{0:T(512)S(1)} %reshape.22.pattern, s32[96]{0:T(128)S(1)} %copy-done.6, bf16[96,64,320]{2,1,0:T(8,128)(2,1)} %coupling.7, f32[96,64,128]{2,1,0:T(8,128)S(1)} %copy-done), custom_call_target="tpu_custom_call" | custom-call | flops 500000000 | bytes 16000000 | tf_op jit(solution)/shard_map/pallas_call | solution.py:240
  100.7 3.3 %reduce_sum.19 = f32[128,64]{1,0:T(8,128)S(1)} reduce(f32[128,64,128]{2,1,0:T(8,128)} %get-tuple-element.42, f32[]{:T(128)} %constant.6.clone.1), dimensions={2}, to_apply=%region_1.2 | reduce | flops 1040384 | bytes 4227076 | tf_op jit(solution)/shard_map/reduce_sum | solution.py:248
  104.1 1.3 collective-permute-start.6
  105.4 2.3 %collective-permute-start.7 = (bf16[128,64]{1,0:T(8,128)(2,1)S(1)}, bf16[128,64]{1,0:T(8,128)(2,1)S(1)}, u32[]{:S(2)}, u32[]{:S(2)}) collective-permute-start(bf16[128,64]{1,0:T(8,128)(2,1)S(1)} %multiply_convert_fusion), channel_id=1, source_target_pairs={{0,16},{8,24},{16,0},{24,8},{1,17},{9,25},{17,1},{25,9},{2,18},{10... | collective-permute-start | bytes 49160 | tf_op jit(solution)/shard_map/ppermute | solution.py:35
  107.7 1.1 collective-permute-start.8
  108.8 0.0 collective-permute-done.6
  108.8 0.3 collective-permute-done.7
  109.1 2.0 %collective-permute-done.8 = bf16[128,64]{1,0:T(8,128)(2,1)S(1)} collective-permute-done((bf16[128,64]{1,0:T(8,128)(2,1)S(1)}, bf16[128,64]{1,0:T(8,128)(2,1)S(1)}, u32[]{:S(2)}, u32[]{:S(2)}) %collective-permute-start.8) | collective-permute-done | bytes 16416 | tf_op jit(solution)/shard_map/ppermute | solution.py:35
  111.1 3.6 %collective-permute-done.5.received = bf16[128,64,128]{2,1,0:T(8,128)(2,1)S(1)} collective-permute-done((bf16[128,64,128]{2,1,0:T(8,128)(2,1)}, bf16[128,64,128]{2,1,0:T(8,128)(2,1)S(1)}, u32[]{:S(2)}, u32[]{:S(2)}) %collective-permute-start.5) | collective-permute-done | bytes 2097184 | tf_op jit(solution)/shard_map/ppermute | solution.py:27
  114.7 1.3 copy-done.10
  116.0 11.4 %shard_map.180 = (f32[128,64,128]{2,1,0:T(8,128)}, bf16[128,64,128]{2,1,0:T(8,128)(2,1)S(1)}, bf16[128,64,128]{2,1,0:T(8,128)(2,1)}) custom-call(s32[128]{0:T(128)S(1)} %copy-done.9, bf16[128,64,128]{2,1,0:T(8,128)(2,1)} %copy-done.10, f32[128,64,128]{2,1,0:T(8,128)} %get-tuple-element.38.grad, f32[128,64,128]{2,1,0:T(8,128)} %get-tuple-element.39.own, ...), custom_call_target="tpu_custom_call" | custom-call | flops 10000000 | bytes 25000000 | tf_op jit(solution)/shard_map/pallas_call | solution.py:178
  127.5 1.9 %collective-permute-start.9 = (bf16[128,64,128]{2,1,0:T(8,128)(2,1)}, bf16[128,64,128]{2,1,0:T(8,128)(2,1)}, u32[]{:S(2)}, u32[]{:S(2)}) collective-permute-start(bf16[128,64,128]{2,1,0:T(8,128)(2,1)} %get-tuple-element.45), channel_id=1, source_target_pairs={{1,0},{2,1},{3,2},{4,3},{5,4},{6,5},{7,6},{9,8},{10,9},{11,10},{12... | collective-permute-start | bytes 6291464 | tf_op jit(solution)/shard_map/ppermute | solution.py:27
  129.4 0.7 copy.35
  130.1 1.6 broadcast_in_dim.8.first
  131.7 0.0 copy-start.3
  131.7 7.1 %shard_map.181 = f32[96,64,128]{2,1,0:T(8,128)} custom-call(s32[1]{0:T(128)S(6)} %copy.36.count, s32[384]{0:T(512)S(1)} %reshape.22.pattern, s32[96]{0:T(128)S(1)} %copy-done.6, bf16[96,64,320]{2,1,0:T(8,128)(2,1)} %coupling.7, bf16[128,64,128]{2,1,0:T(8,128)(2,1)S(1)} %get-tuple-element.46.bar, bf16[128,64,128]{2,1,0:T(8,128)(2,1)S(1)} %broadcast_in_dim.8.first, ...), custom_call_target="tpu_custom_call" | custom-call | flops 500000000 | bytes 18000000 | tf_op jit(solution)/shard_map/pallas_call | solution.py:255
  138.9 16.9 %collective-permute-done.9.arrived = bf16[128,64,128]{2,1,0:T(8,128)(2,1)} collective-permute-done((bf16[128,64,128]{2,1,0:T(8,128)(2,1)}, bf16[128,64,128]{2,1,0:T(8,128)(2,1)}, u32[]{:S(2)}, u32[]{:S(2)}) %collective-permute-start.9) | collective-permute-done | bytes 2097184 | tf_op jit(solution)/shard_map/ppermute | solution.py:27
  155.8 0.0 copy-done.3
  155.8 5.9 %shard_map.182 = f32[128,64,128]{2,1,0:T(8,128)} custom-call(f32[1]{0:T(128)} %bitcast.live, s32[128]{0:T(128)S(1)} %copy-done.8, bf16[128,64,128]{2,1,0:T(8,128)(2,1)S(1)} %copy-done.3, bf16[128,64,128]{2,1,0:T(8,128)(2,1)S(1)} %get-tuple-element.46.bar, bf16[128,64,128]{2,1,0:T(8,128)(2,1)} %collective-permute-done.9.arrived, ...), custom_call_target="tpu_custom_call" | custom-call | flops 600000000 | bytes 18000000 | tf_op jit(solution)/shard_map/pallas_call | solution.py:265
  (16 shorter events, 0.1 us)
Async XLA Ops:
  0.6 1.6 copy-start.1
  2.2 0.7 copy-start.7
  2.9 11.5 %copy-start.15 = (s32[96,4]{0,1:T(4,128)S(1)}, s32[96,4]{0,1:T(4,128)}, u32[]{:S(2)}) copy-start(s32[96,4]{0,1:T(4,128)} %param.17) | copy-start | bytes 4612
  2.9 12.3 %copy-start.4 = (f32[96,64,128]{2,1,0:T(8,128)S(1)}, f32[96,64,128]{2,1,0:T(8,128)}, u32[]{:S(2)}) copy-start(f32[96,64,128]{2,1,0:T(8,128)} %lam.3) | copy-start | bytes 9437188
  2.9 12.3 %copy-start.6 = (s32[96]{0:T(128)S(1)}, s32[96]{0:T(128)}, u32[]{:S(2)}) copy-start(s32[96]{0:T(128)} %link.7) | copy-start | bytes 1156
  9.8 27.8 %collective-permute-start = (bf16[128,64,128]{2,1,0:T(8,128)(2,1)}, bf16[128,64,128]{2,1,0:T(8,128)(2,1)}, u32[]{:S(2)}, u32[]{:S(2)}) collective-permute-start(bf16[128,64,128]{2,1,0:T(8,128)(2,1)} %get-tuple-element.27), channel_id=1, source_target_pairs={{0,1},{1,2},{2,3},{3,4},{4,5},{5,6},{6,7},{8,9},{9,10},{10,11},{11... | collective-permute-start | bytes 6291464 | tf_op jit(solution)/shard_map/ppermute | solution.py:27
  24.5 8.1 %copy-start.11 = (f32[128,64]{0,1:T(8,128)S(1)}, f32[128,64]{0,1:T(8,128)}, u32[]{:S(2)}) copy-start(f32[128,64]{0,1:T(8,128)} %param.23) | copy-start | bytes 98308
  27.9 12.3 %copy-start.9 = (s32[128]{0:T(128)S(1)}, s32[128]{0:T(128)}, u32[]{:S(2)}) copy-start(s32[128]{0:T(128)} %left.3) | copy-start | bytes 1540
  27.9 5.1 %collective-permute-start.1 = (bf16[128,64]{1,0:T(8,128)(2,1)S(1)}, bf16[128,64]{1,0:T(8,128)(2,1)S(1)}, u32[]{:S(2)}, u32[]{:S(2)}) collective-permute-start(bf16[128,64]{1,0:T(8,128)(2,1)S(1)} %multiply_convert_fusion.1), channel_id=1, source_target_pairs={{0,8},{8,16},{16,24},{24,0},{1,9},{9,17},{17,25},{25,1},{2,10},{10... | collective-permute-start | bytes 49160 | tf_op jit(solution)/shard_map/ppermute | solution.py:35
  29.2 4.0 %collective-permute-start.2 = (bf16[128,64]{1,0:T(8,128)(2,1)S(1)}, bf16[128,64]{1,0:T(8,128)(2,1)S(1)}, u32[]{:S(2)}, u32[]{:S(2)}) collective-permute-start(bf16[128,64]{1,0:T(8,128)(2,1)S(1)} %multiply_convert_fusion.1), channel_id=1, source_target_pairs={{0,16},{8,24},{16,0},{24,8},{1,17},{9,25},{17,1},{25,9},{2,18},{10... | collective-permute-start | bytes 49160 | tf_op jit(solution)/shard_map/ppermute | solution.py:35
  31.6 2.8 %collective-permute-start.3 = (bf16[128,64]{1,0:T(8,128)(2,1)S(1)}, bf16[128,64]{1,0:T(8,128)(2,1)S(1)}, u32[]{:S(2)}, u32[]{:S(2)}) collective-permute-start(bf16[128,64]{1,0:T(8,128)(2,1)S(1)} %multiply_convert_fusion.1), channel_id=1, source_target_pairs={{0,24},{8,0},{16,8},{24,16},{1,25},{9,1},{17,9},{25,17},{2,26},{10... | collective-permute-start | bytes 49160 | tf_op jit(solution)/shard_map/ppermute | solution.py:35
  40.2 13.3 %copy-start.12 = (f32[128,64]{0,1:T(8,128)S(1)}, f32[128,64]{0,1:T(8,128)}, u32[]{:S(2)}) copy-start(f32[128,64]{0,1:T(8,128)} %param.22) | copy-start | bytes 98308
  40.2 13.4 %copy-start.13 = (f32[128,64]{0,1:T(8,128)S(1)}, f32[128,64]{0,1:T(8,128)}, u32[]{:S(2)}) copy-start(f32[128,64]{0,1:T(8,128)} %param.26) | copy-start | bytes 98308
  40.2 13.5 %copy-start.14 = (f32[96,64]{0,1:T(8,128)S(1)}, f32[96,64]{0,1:T(8,128)}, u32[]{:S(2)}) copy-start(f32[96,64]{0,1:T(8,128)} %param.24) | copy-start | bytes 73732
  51.6 7.2 %copy-start.5 = (bf16[128,64,128]{2,1,0:T(8,128)(2,1)}, bf16[128,64,128]{2,1,0:T(8,128)(2,1)S(1)}, u32[]{:S(2)}) copy-start(bf16[128,64,128]{2,1,0:T(8,128)(2,1)S(1)} %get-tuple-element.33.bar) | copy-start | bytes 6291460
  51.6 28.4 %collective-permute-start.4 = (bf16[128,64,128]{2,1,0:T(8,128)(2,1)}, bf16[128,64,128]{2,1,0:T(8,128)(2,1)}, u32[]{:S(2)}, u32[]{:S(2)}) collective-permute-start(bf16[128,64,128]{2,1,0:T(8,128)(2,1)} %get-tuple-element.34), channel_id=1, source_target_pairs={{1,0},{2,1},{3,2},{4,3},{5,4},{6,5},{7,6},{9,8},{10,9},{11,10},{12... | collective-permute-start | bytes 6291464 | tf_op jit(solution)/shard_map/ppermute | solution.py:27
  58.7 21.3 %copy-start.2 = (bf16[128,64,128]{2,1,0:T(8,128)(2,1)S(1)}, bf16[128,64,128]{2,1,0:T(8,128)(2,1)}, u32[]{:S(2)}) copy-start(bf16[128,64,128]{2,1,0:T(8,128)(2,1)} %tie.5) | copy-start | bytes 6291460
  58.7 21.2 %copy-start.8 = (s32[128]{0:T(128)S(1)}, s32[128]{0:T(128)}, u32[]{:S(2)}) copy-start(s32[128]{0:T(128)} %right.5) | copy-start | bytes 1540
  65.9 25.5 %copy-start = (f32[96,64,128]{2,1,0:T(8,128)S(1)}, f32[96,64,128]{2,1,0:T(8,128)}, u32[]{:S(2)}) copy-start(f32[96,64,128]{2,1,0:T(8,128)} %shard_map.177.lam) | copy-start | bytes 9437188
  89.5 25.2 %collective-permute-start.5 = (bf16[128,64,128]{2,1,0:T(8,128)(2,1)}, bf16[128,64,128]{2,1,0:T(8,128)(2,1)S(1)}, u32[]{:S(2)}, u32[]{:S(2)}) collective-permute-start(bf16[128,64,128]{2,1,0:T(8,128)(2,1)} %get-tuple-element.36), channel_id=1, source_target_pairs={{0,1},{1,2},{2,3},{3,4},{4,5},{5,6},{6,7},{8,9},{9,10},{10,11},{11... | collective-permute-start | bytes 6291464 | tf_op jit(solution)/shard_map/ppermute | solution.py:27
  104.1 4.7 %collective-permute-start.6 = (bf16[128,64]{1,0:T(8,128)(2,1)S(1)}, bf16[128,64]{1,0:T(8,128)(2,1)S(1)}, u32[]{:S(2)}, u32[]{:S(2)}) collective-permute-start(bf16[128,64]{1,0:T(8,128)(2,1)S(1)} %multiply_convert_fusion), channel_id=1, source_target_pairs={{0,8},{8,16},{16,24},{24,0},{1,9},{9,17},{17,25},{25,1},{2,10},{10... | collective-permute-start | bytes 49160 | tf_op jit(solution)/shard_map/ppermute | solution.py:35
  105.4 3.7 %collective-permute-start.7 = (bf16[128,64]{1,0:T(8,128)(2,1)S(1)}, bf16[128,64]{1,0:T(8,128)(2,1)S(1)}, u32[]{:S(2)}, u32[]{:S(2)}) collective-permute-start(bf16[128,64]{1,0:T(8,128)(2,1)S(1)} %multiply_convert_fusion), channel_id=1, source_target_pairs={{0,16},{8,24},{16,0},{24,8},{1,17},{9,25},{17,1},{25,9},{2,18},{10... | collective-permute-start | bytes 49160 | tf_op jit(solution)/shard_map/ppermute | solution.py:35
  107.7 3.4 %collective-permute-start.8 = (bf16[128,64]{1,0:T(8,128)(2,1)S(1)}, bf16[128,64]{1,0:T(8,128)(2,1)S(1)}, u32[]{:S(2)}, u32[]{:S(2)}) collective-permute-start(bf16[128,64]{1,0:T(8,128)(2,1)S(1)} %multiply_convert_fusion), channel_id=1, source_target_pairs={{0,24},{8,0},{16,8},{24,16},{1,25},{9,1},{17,9},{25,17},{2,26},{10... | collective-permute-start | bytes 49160 | tf_op jit(solution)/shard_map/ppermute | solution.py:35
  114.7 1.3 copy-start.10
  127.5 28.3 %collective-permute-start.9 = (bf16[128,64,128]{2,1,0:T(8,128)(2,1)}, bf16[128,64,128]{2,1,0:T(8,128)(2,1)}, u32[]{:S(2)}, u32[]{:S(2)}) collective-permute-start(bf16[128,64,128]{2,1,0:T(8,128)(2,1)} %get-tuple-element.45), channel_id=1, source_target_pairs={{1,0},{2,1},{3,2},{4,3},{5,4},{6,5},{7,6},{9,8},{10,9},{11,10},{12... | collective-permute-start | bytes 6291464 | tf_op jit(solution)/shard_map/ppermute | solution.py:27
  131.7 24.0 %copy-start.3 = (bf16[128,64,128]{2,1,0:T(8,128)(2,1)S(1)}, bf16[128,64,128]{2,1,0:T(8,128)(2,1)}, u32[]{:S(2)}) copy-start(bf16[128,64,128]{2,1,0:T(8,128)(2,1)} %tie.5) | copy-start | bytes 6291460

commit v4 on v3

--- a/solution.py
+++ b/solution.py
@@ -107,32 +107,44 @@
 
 
 def primal_kernel(left, received, grad, own, cost, second, second_next, second_bar, sent, total):
-    total[...] = grad[...] + own[...]
-
-    def add_step(rows):
-        for j in rows:
-            total[left[j]] += received[j].astype(F32)
-
-    rows_loop(received.shape[0], add_step, 8)
-
-    def move_step(rows):
-        news = []
-        for b in rows:
-            now = second[b]
-            new = jnp.maximum(now - primal_step * (cost[b] - total[b]), 0.0)
-            news.append((new, (2.0 * new - now).astype(BF16)))
-        for b, (new, bar) in zip(rows, news):
-            second_next[b] = new
-            second_bar[b] = bar
-
-    rows_loop(second.shape[0], move_step, 8)
-
-    def gather_step(rows):
-        picked = [second_bar[left[j]] for j in rows]
-        for j, block in zip(rows, picked):
-            sent[j] = block
-
-    rows_loop(received.shape[0], gather_step, 16)
+    at = pl.program_id(0)
+    zero_first(total)
+
+    @pl.when(at < STEPS)
+    def _():
+        base = at * received.shape[0]
+
+        def add_step(rows):
+            for j in rows:
+                total[left[base + j]] += received[j].astype(F32)
+
+        rows_loop(received.shape[0], add_step, 8)
+
+    @pl.when(at >= STEPS)
+    def _():
+        base = (at - STEPS) * second.shape[0]
+
+        def move_step(rows):
+            news = []
+            for b in rows:
+                now = second[b]
+                slope = total[base + b] + grad[b] + own[b]
+                new = jnp.maximum(now - primal_step * (cost[b] - slope), 0.0)
+                news.append((new, (2.0 * new - now).astype(BF16)))
+            for b, (new, bar) in zip(rows, news):
+                second_next[b] = new
+                second_bar[base + b] = bar
+
+        rows_loop(second.shape[0], move_step, 8)
+
+    @pl.when(at == 2 * STEPS - 1)
+    def _():
+        def gather_step(rows):
+            picked = [second_bar[left[j]] for j in rows]
+            for j, block in zip(rows, picked):
+                sent[j] = block
+
+        rows_loop(sent.shape[0], gather_step, 16)
 
 
 def dual_kernel(count, pattern, link, coupling, bar, first, target, lam, lam_next):
@@ -175,15 +187,20 @@
 
 def primal_call(left, received, grad, own, cost, second):
     shape = second.shape
+    arriving = pl.BlockSpec(
+        (received.shape[0] // STEPS,) + received.shape[1:], lambda i: (jnp.minimum(i, STEPS - 1), 0, 0)
+    )
+    moving = pl.BlockSpec((shape[0] // STEPS,) + shape[1:], lambda i: (jnp.maximum(i - STEPS, 0), 0, 0))
     return pl.pallas_call(
         primal_kernel,
+        grid=(2 * STEPS,),
         out_shape=(
             jax.ShapeDtypeStruct(shape, F32),
             jax.ShapeDtypeStruct(shape, BF16),
             jax.ShapeDtypeStruct(received.shape, BF16),
         ),
-        in_specs=[SMEM] + [VMEM] * 5,
-        out_specs=(VMEM,) * 3,
+        in_specs=[SMEM, arriving] + [moving] * 4,
+        out_specs=(moving, resident(shape), resident(received.shape)),
         scratch_shapes=[pltpu.VMEM(shape, F32)],
         compiler_params=pltpu.CompilerParams(vmem_limit_bytes=48 * 2**20),
         cost_estimate=pl.CostEstimate(flops=10**7, bytes_accessed=25 * 10**6, transcendentals=0),
@@ -214,7 +231,6 @@
     wide_shape = commit_start.shape + (scen_dev,)
     live = (lax.axis_index("net") < lax.axis_size("net") - 1).astype(F32).reshape(1)
     pattern = w_pattern.reshape(-1)
-    cost = jnp.broadcast_to(dispatch_cost[:, :, None], second_shape)
     target = demand[:, :, None] + wind_error.astype(F32)
     first_now = commit_start
     second_now = dispatch_start
@@ -235,6 +251,9 @@
         3 * 10**8,
         13 * 10**6,
     )(live, right_bounds, tie_blocks, tie_start)
+    terms, cost_rows = lax.optimization_barrier((terms, dispatch_cost))
+    cost = jnp.broadcast_to(cost_rows[:, :, None], second_shape)
+    cost, dual_now = lax.optimization_barrier((cost, dual_now))
     for iteration in range(ITERS):
         received = from_behind(terms, "net", 1)
         grad, grad_wide = stepped_call(

time: 163 us -> 163 us (level)
  waiting for transfers between devices: 41.7 us -> 38.2 us
  Pallas kernels: 78 us -> 80.1 us
    ppermute x4, waiting for transfers between devices: 37.8 us -> 34.2 us  [from_behind(): return lax.ppermute(value, axis, pairs)]
    pallas_call x2, Pallas kernels: 22.8 us -> 25.3 us  [primal_call(): pl.pallas_call(primal_kernel, grid=(2 * STEPS,), out_shape=(jax.ShapeDtyp...]
    unnamed x38 -> x37, local copies, waits for them, and re-layouts: 4.78 us -> 4.68 us
  transfers between devices with their start and end apart: 10 -> 10, of which waited for: 9 -> 9; matrix products, arithmetic and copies ran while one was open for 9% -> 11% of each run, Pallas kernels for 20% -> 20%
where the time goes in v4:
time: 163 us; the launch traced here: 162 us
  Pallas kernels  80.1 us (49%)
  waiting for transfers between devices  38.2 us (23%)
  starting transfers between devices  21.1 us (13%)
  local copies, waits for them, and re-layouts  10.7 us (7%)
  other arithmetic  10.1 us (6%)
    ppermute x4, waiting for transfers between devices, from_behind(): return lax.ppermute(value, axis, pairs)  34.2 us
    pallas_call x2, Pallas kernels, primal_call(): pl.pallas_call(primal_kernel, grid=(2 * STEPS,), out_shape=(jax.ShapeDtyp...  25.3 us
    pallas_call x2, Pallas kernels, body(): stepped_call(recourse_kernel, (second_f32, jax.ShapeDtypeStruct(wide_shap...  18.4 us
    pallas_call x2, Pallas kernels, body(): stepped_call(tie_kernel, (tie_f32, tie_bf16, second_f32) if more else (ti...  15.3 us
    pallas_call x2, Pallas kernels, body(): stepped_call(dual_kernel, dual_f32, [SMEM] * 3 + [row_mats, seconds, wide...  14.2 us
    ppermute x4, starting transfers between devices, from_behind(): return lax.ppermute(value, axis, pairs)  11.6 us
    ppermute x6, starting transfers between devices, sum_over_scen(): total = total + lax.ppermute(value, 'scen', pairs).astype(F32)  9.46 us
    pallas_call x1, Pallas kernels, body(): stepped_call(start_terms_kernel, (tie_bf16, second_f32), [SMEM, SMEM, tie...  6.77 us
  transfers between devices with their start and end apart: 10, of which 9 were waited for; matrix products, arithmetic and copies ran while one was open for 11% of the time, Pallas kernels for 20%

profile of v4, /device:TPU:1, one launch (start us, length us, event | category | flops | bytes accessed | tf_op | source)
XLA Modules:
  0.0 161.6 jit_solution(17679083449662904084)
XLA Ops:
  0.6 0.0 copy-start.1
  0.6 1.6 copy-done.1
  2.2 0.0 copy-start.7
  2.2 0.7 copy-done.7
  2.9 0.0 copy-start.11
  2.9 6.8 %shard_map.174 = (bf16[128,64,128]{2,1,0:T(8,128)(2,1)}, f32[128,64,128]{2,1,0:T(8,128)}) custom-call(f32[1]{0:T(128)} %bitcast.live, s32[128]{0:T(128)S(1)} %copy-done.7, bf16[128,64,128]{2,1,0:T(8,128)(2,1)S(1)} %copy-done.1, f32[128,64,128]{2,1,0:T(8,128)} %mu.3), custom_call_target="tpu_custom_call" | custom-call | flops 300000000 | bytes 13000000 | tf_op jit(solution)/shard_map/pallas_call | solution.py:246
  9.7 4.8 %collective-permute-start = (bf16[128,64,128]{2,1,0:T(8,128)(2,1)}, bf16[128,64,128]{2,1,0:T(8,128)(2,1)}, u32[]{:S(2)}, u32[]{:S(2)}) collective-permute-start(bf16[128,64,128]{2,1,0:T(8,128)(2,1)} %get-tuple-element.32), channel_id=1, source_target_pairs={{0,1},{1,2},{2,3},{3,4},{4,5},{5,6},{6,7},{8,9},{9,10},{10,11},{11... | collective-permute-start | bytes 6291464 | tf_op jit(solution)/shard_map/ppermute | solution.py:27
  14.4 0.0 copy-done.11
  14.5 0.1 copy.29
  14.6 2.6 %broadcast_in_dim.6.cost = f32[128,64,128]{2,1,0:T(8,128)} broadcast(f32[128,64]{1,0:T(8,128)S(1)} %copy.29), dimensions={0,1} | broadcast | bytes 4227072 | tf_op jit(solution)/shard_map/broadcast_in_dim | solution.py:255
  17.1 0.0 copy-done.15
  17.1 0.1 copy.28
  17.2 0.1 reshape.22.pattern
  18.0 0.0 copy-done.4
  18.0 0.0 copy-done.6
  18.0 9.2 %shard_map.175 = (f32[128,64,128]{2,1,0:T(8,128)}, f32[128,64,128]{2,1,0:T(8,128)}) custom-call(s32[1]{0:T(128)S(6)} %copy.36.count, s32[384]{0:T(512)S(1)} %reshape.22.pattern, s32[96]{0:T(128)S(1)} %copy-done.6, bf16[96,64,320]{2,1,0:T(8,128)(2,1)} %coupling.7, f32[96,64,128]{2,1,0:T(8,128)S(1)} %copy-done.4), custom_call_target="tpu_custom_call" | custom-call | flops 500000000 | bytes 16000000 | tf_op jit(solution)/shard_map/pallas_call | solution.py:259
  27.3 3.3 %reduce_sum.18 = f32[128,64]{1,0:T(8,128)S(1)} reduce(f32[128,64,128]{2,1,0:T(8,128)} %get-tuple-element.39, f32[]{:T(128)} %constant.6.clone.1), dimensions={2}, to_apply=%region_0.0 | reduce | flops 1040384 | bytes 4227076 | tf_op jit(solution)/shard_map/reduce_sum | solution.py:267
  30.6 1.3 collective-permute-start.1
  32.0 2.3 %collective-permute-start.2 = (bf16[128,64]{1,0:T(8,128)(2,1)S(1)}, bf16[128,64]{1,0:T(8,128)(2,1)S(1)}, u32[]{:S(2)}, u32[]{:S(2)}) collective-permute-start(bf16[128,64]{1,0:T(8,128)(2,1)S(1)} %multiply_convert_fusion.1), channel_id=1, source_target_pairs={{0,16},{8,24},{16,0},{24,8},{1,17},{9,25},{17,1},{25,9},{2,18},{10... | collective-permute-start | bytes 49160 | tf_op jit(solution)/shard_map/ppermute | solution.py:35
  34.3 1.1 collective-permute-start.3
  35.4 0.4 collective-permute-done.1
  35.7 0.3 collective-permute-done.2
  36.0 1.1 collective-permute-done.3
  37.1 0.6 collective-permute-done.received
  37.7 0.0 copy-done.9
  37.7 12.7 %shard_map.176 = (f32[128,64,128]{2,1,0:T(8,128)}, bf16[128,64,128]{2,1,0:T(8,128)(2,1)S(1)}, bf16[128,64,128]{2,1,0:T(8,128)(2,1)}) custom-call(s32[128]{0:T(128)S(1)} %copy-done.9, bf16[128,64,128]{2,1,0:T(8,128)(2,1)} %collective-permute-done.received, f32[128,64,128]{2,1,0:T(8,128)} %get-tuple-element.35.grad, f32[128,64,128]{2,1,0:T(8,128)} %get-tuple-element.36.own, ...), custom_call_target="tpu_custom_call" | custom-call | flops 10000000 | bytes 25000000 | tf_op jit(solution)/shard_map/pallas_call | solution.py:194
  50.4 3.0 %collective-permute-start.4 = (bf16[128,64,128]{2,1,0:T(8,128)(2,1)}, bf16[128,64,128]{2,1,0:T(8,128)(2,1)}, u32[]{:S(2)}, u32[]{:S(2)}) collective-permute-start(bf16[128,64,128]{2,1,0:T(8,128)(2,1)} %get-tuple-element.42), channel_id=1, source_target_pairs={{1,0},{2,1},{3,2},{4,3},{5,4},{6,5},{7,6},{9,8},{10,9},{11,10},{12... | collective-permute-start | bytes 6291464 | tf_op jit(solution)/shard_map/ppermute | solution.py:27
  53.4 0.0 copy-done.12
  53.4 0.1 copy.30
  53.5 0.0 copy-done.13
  53.6 0.1 copy.31
  53.6 0.0 copy-done.14
  53.7 0.1 copy.33
  53.7 3.3 %convert_add_fusion.target = f32[96,64,128]{2,1,0:T(8,128)} fusion(bf16[96,64,128]{2,1,0:T(8,128)(2,1)} %param.25, f32[96,64]{1,0:T(8,128)S(1)} %copy.33), kind=kLoop, calls=%fused_computation | loop fusion | flops 1572864 | bytes 4743168 | tf_op jit(solution)/shard_map/add | solution.py:234
  57.0 1.6 %broadcast_in_dim.7.first = bf16[128,64,128]{2,1,0:T(8,128)(2,1)S(1)} broadcast(bf16[128,64]{1,0:T(8,128)(2,1)S(1)} %subtract_convert_fusion.1), dimensions={0,1} | broadcast | bytes 2113536 | tf_op jit(solution)/shard_map/broadcast_in_dim | solution.py:273
  58.7 0.0 copy-done.5
  58.7 0.0 copy-start.2
  58.7 0.0 copy-start.8
  58.7 7.1 %shard_map.177.lam = f32[96,64,128]{2,1,0:T(8,128)} custom-call(s32[1]{0:T(128)S(6)} %copy.36.count, s32[384]{0:T(512)S(1)} %reshape.22.pattern, s32[96]{0:T(128)S(1)} %copy-done.6, bf16[96,64,320]{2,1,0:T(8,128)(2,1)} %coupling.7, bf16[128,64,128]{2,1,0:T(8,128)(2,1)S(1)} %get-tuple-element.41.bar, bf16[128,64,128]{2,1,0:T(8,128)(2,1)S(1)} %broadcast_in_dim.7.first, ...), custom_call_target="tpu_custom_call" | custom-call | flops 500000000 | bytes 18000000 | tf_op jit(solution)/shard_map/pallas_call | solution.py:274
  65.8 13.0 %collective-permute-done.4.arrived = bf16[128,64,128]{2,1,0:T(8,128)(2,1)} collective-permute-done((bf16[128,64,128]{2,1,0:T(8,128)(2,1)}, bf16[128,64,128]{2,1,0:T(8,128)(2,1)}, u32[]{:S(2)}, u32[]{:S(2)}) %collective-permute-start.4) | collective-permute-done | bytes 2097184 | tf_op jit(solution)/shard_map/ppermute | solution.py:27
  78.8 0.0 copy-done.2
  78.8 0.0 copy-done.8
  78.8 9.4 %shard_map.178 = (f32[128,64,128]{2,1,0:T(8,128)}, bf16[128,64,128]{2,1,0:T(8,128)(2,1)}, f32[128,64,128]{2,1,0:T(8,128)}) custom-call(f32[1]{0:T(128)} %bitcast.live, s32[128]{0:T(128)S(1)} %copy-done.8, bf16[128,64,128]{2,1,0:T(8,128)(2,1)S(1)} %copy-done.2, bf16[128,64,128]{2,1,0:T(8,128)(2,1)} %copy-done.5, ...), custom_call_target="tpu_custom_call" | custom-call | flops 600000000 | bytes 18000000 | tf_op jit(solution)/shard_map/pallas_call | solution.py:284
  88.3 1.9 %collective-permute-start.5 = (bf16[128,64,128]{2,1,0:T(8,128)(2,1)}, bf16[128,64,128]{2,1,0:T(8,128)(2,1)S(1)}, u32[]{:S(2)}, u32[]{:S(2)}) collective-permute-start(bf16[128,64,128]{2,1,0:T(8,128)(2,1)} %get-tuple-element.44), channel_id=1, source_target_pairs={{0,1},{1,2},{2,3},{3,4},{4,5},{5,6},{6,7},{8,9},{9,10},{10,11},{11... | collective-permute-start | bytes 6291464 | tf_op jit(solution)/shard_map/ppermute | solution.py:27
  90.2 0.0 copy-done
  90.2 9.2 %shard_map.179 = (f32[128,64,128]{2,1,0:T(8,128)}, f32[128,64,128]{2,1,0:T(8,128)}) custom-call(s32[1]{0:T(128)S(6)} %copy.36.count, s32[384]{0:T(512)S(1)} %reshape.22.pattern, s32[96]{0:T(128)S(1)} %copy-done.6, bf16[96,64,320]{2,1,0:T(8,128)(2,1)} %coupling.7, f32[96,64,128]{2,1,0:T(8,128)S(1)} %copy-done), custom_call_target="tpu_custom_call" | custom-call | flops 500000000 | bytes 16000000 | tf_op jit(solution)/shard_map/pallas_call | solution.py:259
  99.4 3.3 %reduce_sum.19 = f32[128,64]{1,0:T(8,128)S(1)} reduce(f32[128,64,128]{2,1,0:T(8,128)} %get-tuple-element.50, f32[]{:T(128)} %constant.6.clone.1), dimensions={2}, to_apply=%region_1.2 | reduce | flops 1040384 | bytes 4227076 | tf_op jit(solution)/shard_map/reduce_sum | solution.py:267
  102.7 1.4 collective-permute-start.6
  104.1 2.3 %collective-permute-start.7 = (bf16[128,64]{1,0:T(8,128)(2,1)S(1)}, bf16[128,64]{1,0:T(8,128)(2,1)S(1)}, u32[]{:S(2)}, u32[]{:S(2)}) collective-permute-start(bf16[128,64]{1,0:T(8,128)(2,1)S(1)} %multiply_convert_fusion), channel_id=1, source_target_pairs={{0,16},{8,24},{16,0},{24,8},{1,17},{9,25},{17,1},{25,9},{2,18},{10... | collective-permute-start | bytes 49160 | tf_op jit(solution)/shard_map/ppermute | solution.py:35
  106.4 1.1 collective-permute-start.8
  107.5 0.0 collective-permute-done.6
  107.5 0.3 collective-permute-done.7
  107.8 2.0 %collective-permute-done.8 = bf16[128,64]{1,0:T(8,128)(2,1)S(1)} collective-permute-done((bf16[128,64]{1,0:T(8,128)(2,1)S(1)}, bf16[128,64]{1,0:T(8,128)(2,1)S(1)}, u32[]{:S(2)}, u32[]{:S(2)}) %collective-permute-start.8) | collective-permute-done | bytes 16416 | tf_op jit(solution)/shard_map/ppermute | solution.py:35
  109.8 3.6 %collective-permute-done.5.received = bf16[128,64,128]{2,1,0:T(8,128)(2,1)S(1)} collective-permute-done((bf16[128,64,128]{2,1,0:T(8,128)(2,1)}, bf16[128,64,128]{2,1,0:T(8,128)(2,1)S(1)}, u32[]{:S(2)}, u32[]{:S(2)}) %collective-permute-start.5) | collective-permute-done | bytes 2097184 | tf_op jit(solution)/shard_map/ppermute | solution.py:27
  113.4 1.3 copy-done.10
  114.8 12.7 %shard_map.180 = (f32[128,64,128]{2,1,0:T(8,128)}, bf16[128,64,128]{2,1,0:T(8,128)(2,1)S(1)}, bf16[128,64,128]{2,1,0:T(8,128)(2,1)}) custom-call(s32[128]{0:T(128)S(1)} %copy-done.9, bf16[128,64,128]{2,1,0:T(8,128)(2,1)} %copy-done.10, f32[128,64,128]{2,1,0:T(8,128)} %get-tuple-element.46.grad, f32[128,64,128]{2,1,0:T(8,128)} %get-tuple-element.47.own, ...), custom_call_target="tpu_custom_call" | custom-call | flops 10000000 | bytes 25000000 | tf_op jit(solution)/shard_map/pallas_call | solution.py:194
  127.5 1.9 %collective-permute-start.9 = (bf16[128,64,128]{2,1,0:T(8,128)(2,1)}, bf16[128,64,128]{2,1,0:T(8,128)(2,1)}, u32[]{:S(2)}, u32[]{:S(2)}) collective-permute-start(bf16[128,64,128]{2,1,0:T(8,128)(2,1)} %get-tuple-element.53), channel_id=1, source_target_pairs={{1,0},{2,1},{3,2},{4,3},{5,4},{6,5},{7,6},{9,8},{10,9},{11,10},{12... | collective-permute-start | bytes 6291464 | tf_op jit(solution)/shard_map/ppermute | solution.py:27
  129.4 0.7 copy.35
  130.1 1.6 broadcast_in_dim.8.first
  131.7 0.0 copy-start.3
  131.7 7.1 %shard_map.181 = f32[96,64,128]{2,1,0:T(8,128)} custom-call(s32[1]{0:T(128)S(6)} %copy.36.count, s32[384]{0:T(512)S(1)} %reshape.22.pattern, s32[96]{0:T(128)S(1)} %copy-done.6, bf16[96,64,320]{2,1,0:T(8,128)(2,1)} %coupling.7, bf16[128,64,128]{2,1,0:T(8,128)(2,1)S(1)} %get-tuple-element.54.bar, bf16[128,64,128]{2,1,0:T(8,128)(2,1)S(1)} %broadcast_in_dim.8.first, ...), custom_call_target="tpu_custom_call" | custom-call | flops 500000000 | bytes 18000000 | tf_op jit(solution)/shard_map/pallas_call | solution.py:274
  138.8 16.9 %collective-permute-done.9.arrived = bf16[128,64,128]{2,1,0:T(8,128)(2,1)} collective-permute-done((bf16[128,64,128]{2,1,0:T(8,128)(2,1)}, bf16[128,64,128]{2,1,0:T(8,128)(2,1)}, u32[]{:S(2)}, u32[]{:S(2)}) %collective-permute-start.9) | collective-permute-done | bytes 2097184 | tf_op jit(solution)/shard_map/ppermute | solution.py:27
  155.8 0.0 copy-done.3
  155.8 5.9 %shard_map.182 = f32[128,64,128]{2,1,0:T(8,128)} custom-call(f32[1]{0:T(128)} %bitcast.live, s32[128]{0:T(128)S(1)} %copy-done.8, bf16[128,64,128]{2,1,0:T(8,128)(2,1)S(1)} %copy-done.3, bf16[128,64,128]{2,1,0:T(8,128)(2,1)S(1)} %get-tuple-element.54.bar, bf16[128,64,128]{2,1,0:T(8,128)(2,1)} %collective-permute-done.9.arrived, ...), custom_call_target="tpu_custom_call" | custom-call | flops 600000000 | bytes 18000000 | tf_op jit(solution)/shard_map/pallas_call | solution.py:284
  (16 shorter events, 0.1 us)
Async XLA Ops:
  0.6 1.6 copy-start.1
  2.2 0.7 copy-start.7
  2.9 11.6 %copy-start.11 = (f32[128,64]{0,1:T(8,128)S(1)}, f32[128,64]{0,1:T(8,128)}, u32[]{:S(2)}) copy-start(f32[128,64]{0,1:T(8,128)} %param.23) | copy-start | bytes 98308
  9.7 7.5 %copy-start.15 = (s32[96,4]{0,1:T(4,128)S(1)}, s32[96,4]{0,1:T(4,128)}, u32[]{:S(2)}) copy-start(s32[96,4]{0,1:T(4,128)} %param.17) | copy-start | bytes 4612
  9.7 8.3 %copy-start.4 = (f32[96,64,128]{2,1,0:T(8,128)S(1)}, f32[96,64,128]{2,1,0:T(8,128)}, u32[]{:S(2)}) copy-start(f32[96,64,128]{2,1,0:T(8,128)} %lam.1) | copy-start | bytes 9437188
  9.7 8.4 %copy-start.6 = (s32[96]{0:T(128)S(1)}, s32[96]{0:T(128)}, u32[]{:S(2)}) copy-start(s32[96]{0:T(128)} %link.7) | copy-start | bytes 1156
  9.7 28.1 %collective-permute-start = (bf16[128,64,128]{2,1,0:T(8,128)(2,1)}, bf16[128,64,128]{2,1,0:T(8,128)(2,1)}, u32[]{:S(2)}, u32[]{:S(2)}) collective-permute-start(bf16[128,64,128]{2,1,0:T(8,128)(2,1)} %get-tuple-element.32), channel_id=1, source_target_pairs={{0,1},{1,2},{2,3},{3,4},{4,5},{5,6},{6,7},{8,9},{9,10},{10,11},{11... | collective-permute-start | bytes 6291464 | tf_op jit(solution)/shard_map/ppermute | solution.py:27
  27.3 10.5 %copy-start.9 = (s32[128]{0:T(128)S(1)}, s32[128]{0:T(128)}, u32[]{:S(2)}) copy-start(s32[128]{0:T(128)} %left.3) | copy-start | bytes 1540
  30.6 5.1 %collective-permute-start.1 = (bf16[128,64]{1,0:T(8,128)(2,1)S(1)}, bf16[128,64]{1,0:T(8,128)(2,1)S(1)}, u32[]{:S(2)}, u32[]{:S(2)}) collective-permute-start(bf16[128,64]{1,0:T(8,128)(2,1)S(1)} %multiply_convert_fusion.1), channel_id=1, source_target_pairs={{0,8},{8,16},{16,24},{24,0},{1,9},{9,17},{17,25},{25,1},{2,10},{10... | collective-permute-start | bytes 49160 | tf_op jit(solution)/shard_map/ppermute | solution.py:35
  32.0 4.0 %collective-permute-start.2 = (bf16[128,64]{1,0:T(8,128)(2,1)S(1)}, bf16[128,64]{1,0:T(8,128)(2,1)S(1)}, u32[]{:S(2)}, u32[]{:S(2)}) collective-permute-start(bf16[128,64]{1,0:T(8,128)(2,1)S(1)} %multiply_convert_fusion.1), channel_id=1, source_target_pairs={{0,16},{8,24},{16,0},{24,8},{1,17},{9,25},{17,1},{25,9},{2,18},{10... | collective-permute-start | bytes 49160 | tf_op jit(solution)/shard_map/ppermute | solution.py:35
  34.3 2.8 %collective-permute-start.3 = (bf16[128,64]{1,0:T(8,128)(2,1)S(1)}, bf16[128,64]{1,0:T(8,128)(2,1)S(1)}, u32[]{:S(2)}, u32[]{:S(2)}) collective-permute-start(bf16[128,64]{1,0:T(8,128)(2,1)S(1)} %multiply_convert_fusion.1), channel_id=1, source_target_pairs={{0,24},{8,0},{16,8},{24,16},{1,25},{9,1},{17,9},{25,17},{2,26},{10... | collective-permute-start | bytes 49160 | tf_op jit(solution)/shard_map/ppermute | solution.py:35
  37.7 15.7 %copy-start.12 = (f32[128,64]{0,1:T(8,128)S(1)}, f32[128,64]{0,1:T(8,128)}, u32[]{:S(2)}) copy-start(f32[128,64]{0,1:T(8,128)} %param.22) | copy-start | bytes 98308
  37.7 15.8 %copy-start.13 = (f32[128,64]{0,1:T(8,128)S(1)}, f32[128,64]{0,1:T(8,128)}, u32[]{:S(2)}) copy-start(f32[128,64]{0,1:T(8,128)} %param.26) | copy-start | bytes 98308
  37.7 15.9 %copy-start.14 = (f32[96,64]{0,1:T(8,128)S(1)}, f32[96,64]{0,1:T(8,128)}, u32[]{:S(2)}) copy-start(f32[96,64]{0,1:T(8,128)} %param.24) | copy-start | bytes 73732
  50.4 8.3 %copy-start.5 = (bf16[128,64,128]{2,1,0:T(8,128)(2,1)}, bf16[128,64,128]{2,1,0:T(8,128)(2,1)S(1)}, u32[]{:S(2)}) copy-start(bf16[128,64,128]{2,1,0:T(8,128)(2,1)S(1)} %get-tuple-element.41.bar) | copy-start | bytes 6291460
  50.4 28.4 %collective-permute-start.4 = (bf16[128,64,128]{2,1,0:T(8,128)(2,1)}, bf16[128,64,128]{2,1,0:T(8,128)(2,1)}, u32[]{:S(2)}, u32[]{:S(2)}) collective-permute-start(bf16[128,64,128]{2,1,0:T(8,128)(2,1)} %get-tuple-element.42), channel_id=1, source_target_pairs={{1,0},{2,1},{3,2},{4,3},{5,4},{6,5},{7,6},{9,8},{10,9},{11,10},{12... | collective-permute-start | bytes 6291464 | tf_op jit(solution)/shard_map/ppermute | solution.py:27
  58.7 20.1 %copy-start.2 = (bf16[128,64,128]{2,1,0:T(8,128)(2,1)S(1)}, bf16[128,64,128]{2,1,0:T(8,128)(2,1)}, u32[]{:S(2)}) copy-start(bf16[128,64,128]{2,1,0:T(8,128)(2,1)} %tie.5) | copy-start | bytes 6291460
  58.7 20.1 %copy-start.8 = (s32[128]{0:T(128)S(1)}, s32[128]{0:T(128)}, u32[]{:S(2)}) copy-start(s32[128]{0:T(128)} %right.5) | copy-start | bytes 1540
  65.8 24.3 %copy-start = (f32[96,64,128]{2,1,0:T(8,128)S(1)}, f32[96,64,128]{2,1,0:T(8,128)}, u32[]{:S(2)}) copy-start(f32[96,64,128]{2,1,0:T(8,128)} %shard_map.177.lam) | copy-start | bytes 9437188
  88.3 25.2 %collective-permute-start.5 = (bf16[128,64,128]{2,1,0:T(8,128)(2,1)}, bf16[128,64,128]{2,1,0:T(8,128)(2,1)S(1)}, u32[]{:S(2)}, u32[]{:S(2)}) collective-permute-start(bf16[128,64,128]{2,1,0:T(8,128)(2,1)} %get-tuple-element.44), channel_id=1, source_target_pairs={{0,1},{1,2},{2,3},{3,4},{4,5},{5,6},{6,7},{8,9},{9,10},{10,11},{11... | collective-permute-start | bytes 6291464 | tf_op jit(solution)/shard_map/ppermute | solution.py:27
  102.7 4.7 %collective-permute-start.6 = (bf16[128,64]{1,0:T(8,128)(2,1)S(1)}, bf16[128,64]{1,0:T(8,128)(2,1)S(1)}, u32[]{:S(2)}, u32[]{:S(2)}) collective-permute-start(bf16[128,64]{1,0:T(8,128)(2,1)S(1)} %multiply_convert_fusion), channel_id=1, source_target_pairs={{0,8},{8,16},{16,24},{24,0},{1,9},{9,17},{17,25},{25,1},{2,10},{10... | collective-permute-start | bytes 49160 | tf_op jit(solution)/shard_map/ppermute | solution.py:35
  104.1 3.7 %collective-permute-start.7 = (bf16[128,64]{1,0:T(8,128)(2,1)S(1)}, bf16[128,64]{1,0:T(8,128)(2,1)S(1)}, u32[]{:S(2)}, u32[]{:S(2)}) collective-permute-start(bf16[128,64]{1,0:T(8,128)(2,1)S(1)} %multiply_convert_fusion), channel_id=1, source_target_pairs={{0,16},{8,24},{16,0},{24,8},{1,17},{9,25},{17,1},{25,9},{2,18},{10... | collective-permute-start | bytes 49160 | tf_op jit(solution)/shard_map/ppermute | solution.py:35
  106.4 3.4 %collective-permute-start.8 = (bf16[128,64]{1,0:T(8,128)(2,1)S(1)}, bf16[128,64]{1,0:T(8,128)(2,1)S(1)}, u32[]{:S(2)}, u32[]{:S(2)}) collective-permute-start(bf16[128,64]{1,0:T(8,128)(2,1)S(1)} %multiply_convert_fusion), channel_id=1, source_target_pairs={{0,24},{8,0},{16,8},{24,16},{1,25},{9,1},{17,9},{25,17},{2,26},{10... | collective-permute-start | bytes 49160 | tf_op jit(solution)/shard_map/ppermute | solution.py:35
  113.4 1.3 copy-start.10
  127.5 28.3 %collective-permute-start.9 = (bf16[128,64,128]{2,1,0:T(8,128)(2,1)}, bf16[128,64,128]{2,1,0:T(8,128)(2,1)}, u32[]{:S(2)}, u32[]{:S(2)}) collective-permute-start(bf16[128,64,128]{2,1,0:T(8,128)(2,1)} %get-tuple-element.53), channel_id=1, source_target_pairs={{1,0},{2,1},{3,2},{4,3},{5,4},{6,5},{7,6},{9,8},{10,9},{11,10},{12... | collective-permute-start | bytes 6291464 | tf_op jit(solution)/shard_map/ppermute | solution.py:27
  131.7 24.0 %copy-start.3 = (bf16[128,64,128]{2,1,0:T(8,128)(2,1)S(1)}, bf16[128,64,128]{2,1,0:T(8,128)(2,1)}, u32[]{:S(2)}) copy-start(bf16[128,64,128]{2,1,0:T(8,128)(2,1)} %tie.5) | copy-start | bytes 6291460
